TPU v7x, 32 devices: a whole 2x2x4 slice. The times are simulated.
32 devices in a mesh: dp: 4 (over y, x), blk: 8 (over z, core).
Axes of the slice: x: 2, y: 2, z: 4, core: 2. Of those that a mesh axis runs over, the one named last changes fastest.
Arguments:
- target: bfloat16 [16, 2048, 512], P('dp', 'blk'), may hold values from -6 to 6
- memory: bfloat16 [16, 2048, 512], P('dp', 'blk'), may hold values from -6 to 6
- target_seg: int32 [16, 2048], P('dp', 'blk'), may hold values from 0 to 2, as said below
- target_keep: int32 [16, 2048], P('dp', 'blk'), may hold values from 0 to 1, as said below
- memory_seg: int32 [16, 2048], P('dp', 'blk'), may hold values from 0 to 2, as said below
- memory_keep: int32 [16, 2048], P('dp', 'blk'), may hold values from 0 to 1, as said below
- cotangent: bfloat16 [16, 2048, 512], P('dp', 'blk'), may hold values from -6 to 6
- norm1_gain: float32 [512], replicated, may hold values from 0.5 to 1.5
- norm1_bias: float32 [512], replicated, may hold values from -3 to 3
- w_qkv: bfloat16 [512, 1536], replicated, may hold values from -0.25 to 0.25
- w_out: bfloat16 [512, 512], replicated, may hold values from -3 to 3
- norm2_gain: float32 [512], replicated, may hold values from 0.5 to 1.5
- norm2_bias: float32 [512], replicated, may hold values from -3 to 3
- w_cross_q: bfloat16 [512, 512], replicated, may hold values from -0.25 to 0.25
- w_cross_kv: bfloat16 [512, 1024], replicated, may hold values from -0.25 to 0.25
- w_cross_out: bfloat16 [512, 512], replicated, may hold values from -3 to 3
- norm3_gain: float32 [512], replicated, may hold values from 0.5 to 1.5
- norm3_bias: float32 [512], replicated, may hold values from -3 to 3
- w_up: bfloat16 [512, 2048], replicated, may hold values from -0.25 to 0.25
- b_up: float32 [2048], replicated, may hold values from -3 to 3
- w_down: bfloat16 [2048, 512], replicated, may hold values from -0.125 to 0.125
- b_down: float32 [512], replicated, may hold values from -2 to 2
Outputs:
- block_out: float32 [16, 2048, 512], P('dp', 'blk')
- target_grad: float32 [16, 2048, 512], P('dp', 'blk')
- memory_grad: float32 [16, 2048, 512], P('dp', 'blk')
- grad_norm1_gain: float32 [512], replicated
- grad_norm1_bias: float32 [512], replicated
- grad_w_qkv: float32 [512, 1536], replicated
- grad_w_out: float32 [512, 512], replicated
- grad_norm2_gain: float32 [512], replicated
- grad_norm2_bias: float32 [512], replicated
- grad_w_cross_q: float32 [512, 512], replicated
- grad_w_cross_kv: float32 [512, 1024], replicated
- grad_w_cross_out: float32 [512, 512], replicated
- grad_norm3_gain: float32 [512], replicated
- grad_norm3_bias: float32 [512], replicated
- grad_w_up: float32 [512, 2048], replicated
- grad_b_up: float32 [2048], replicated
- grad_w_down: float32 [2048, 512], replicated
- grad_b_down: float32 [512], replicated
Inputs may be any that keep to these rules, and one draw needn't show every extreme that they name: `target_seg`: within a row, pair numbers never fall and every pair 0, 1, 2 is present; pair 1 runs from inside the first 256 tokens to inside the last 256. `target_keep`: padding is a run of one or more tokens at the end of each row, inside its pair 2, which keeps a real token. `memory_seg`: within a row, pair numbers never fall and every pair 0, 1, 2 is present; pair 1 runs from inside the first 256 tokens to inside the last 256. `memory_keep`: padding is a run of one or more tokens at the end of each row, inside its pair 2, which keeps a real token.
All inputs are finite; a program needn't handle non-finite values.
Results may differ from a plain program's by a relative error of at most 0.03.
Values may be sent and summed in bfloat16 or wider, within the bound.
No kernel may reach another device: no remote copies, remote signals or barrier semaphores. Data moves between devices by JAX's collectives and lax.ppermute only.
A program may use at most 256 MiB of HBM per device.

v0:
```python
import jax
import jax.numpy as jnp
from jax import lax
from jax.sharding import PartitionSpec as P

HEADS = 8


def layer_norm(values, scale_gain, shift_bias):
    centered = values - jnp.mean(values, axis=-1, keepdims=True)
    spread = jnp.mean(centered * centered, axis=-1, keepdims=True)
    return centered * lax.rsqrt(spread + 1e-05) * scale_gain + shift_bias


def split_heads(values):
    return values.reshape(values.shape[0], values.shape[1], HEADS, values.shape[2] // HEADS)


def block_scores(queries, keys_now, query_seg, key_code):
    head_size = queries.shape[-1] // HEADS
    scores = jnp.einsum(
        "sqhd,skhd->shqk",
        split_heads(queries),
        split_heads(keys_now),
        preferred_element_type=jnp.float32,
    ) * head_size ** (-0.5)
    allowed = query_seg[:, None, :, None] == key_code[:, None, None, :]
    return (scores, allowed)


def start_state(queries):
    groups, length, features = queries.shape
    return (
        jnp.full((groups, HEADS, length), -1e30, jnp.float32),
        jnp.zeros((groups, HEADS, length), jnp.float32),
        jnp.zeros((groups, length, HEADS, features // HEADS), jnp.float32),
    )


def fold_keys(queries, query_seg):
    features = queries.shape[-1]

    def absorb(running, portion, offset):
        largest, running_sum, weighted = running
        keyvals, key_code = portion
        scores, allowed = block_scores(queries, keyvals[..., :features], query_seg, key_code)
        newest = jnp.maximum(largest, jnp.max(jnp.where(allowed, scores, -1e30), axis=-1))
        weights = jnp.where(allowed, jnp.exp(scores - newest[..., None]), 0.0)
        factor = jnp.exp(largest - newest)
        running_sum = running_sum * factor + jnp.sum(weights, axis=-1)
        update = jnp.einsum(
            "shqk,skhd->sqhd",
            weights.astype(jnp.bfloat16),
            split_heads(keyvals[..., features:]),
            preferred_element_type=jnp.float32,
        )
        weighted = weighted * jnp.transpose(factor, (0, 2, 1))[..., None] + update
        return (newest, running_sum, weighted)

    return absorb


def finish_state(running):
    largest, running_sum, weighted = running
    outputs = weighted / jnp.transpose(running_sum, (0, 2, 1))[..., None]
    groups, length = (outputs.shape[0], outputs.shape[1])
    return (outputs.reshape(groups, length, -1), largest + jnp.log(running_sum))


def attend_local(queries, query_seg, keyvals, key_codes):
    absorb = fold_keys(queries, query_seg)
    block_len = min(512, keyvals.shape[1])
    block_count = keyvals.shape[1] // block_len

    def advance(block_index, running):
        offset = block_index * block_len
        portion = (
            lax.dynamic_slice_in_dim(keyvals, offset, block_len, 1),
            lax.dynamic_slice_in_dim(key_codes, offset, block_len, 1),
        )
        return absorb(running, portion, offset)

    return finish_state(lax.fori_loop(0, block_count, advance, start_state(queries)))


def attend_back(queries, query_seg, grad_heads_low, log_sums, deltas, keyvals, key_codes):
    groups, length, features = queries.shape
    head_size = features // HEADS
    score_scale = head_size ** (-0.5)
    block_len = min(512, keyvals.shape[1])
    block_count = keyvals.shape[1] // block_len
    grad_heads = split_heads(grad_heads_low)
    query_heads = split_heads(queries)

    def advance(block_index, running):
        grad_query, grad_keyvals = running
        offset = block_index * block_len
        kv_block = lax.dynamic_slice_in_dim(keyvals, offset, block_len, 1)
        code_block = lax.dynamic_slice_in_dim(key_codes, offset, block_len, 1)
        scores, allowed = block_scores(queries, kv_block[..., :features], query_seg, code_block)
        probability = jnp.where(allowed, jnp.exp(scores - log_sums[..., None]), 0.0)
        grad_probs = jnp.einsum(
            "sqhd,skhd->shqk",
            grad_heads,
            split_heads(kv_block[..., features:]),
            preferred_element_type=jnp.float32,
        )
        grad_scores = (probability * (grad_probs - deltas[..., None])).astype(jnp.bfloat16)
        grad_query = (
            grad_query
            + jnp.einsum(
                "shqk,skhd->sqhd",
                grad_scores,
                split_heads(kv_block[..., :features]),
                preferred_element_type=jnp.float32,
            )
            * score_scale
        )
        grad_values = jnp.einsum(
            "shqk,sqhd->skhd",
            probability.astype(jnp.bfloat16),
            grad_heads,
            preferred_element_type=jnp.float32,
        )
        grad_keys = (
            jnp.einsum(
                "shqk,sqhd->skhd", grad_scores, query_heads, preferred_element_type=jnp.float32
            )
            * score_scale
        )
        joined = jnp.concatenate(
            [
                grad_keys.reshape(groups, block_len, features),
                grad_values.reshape(groups, block_len, features),
            ],
            axis=-1,
        )
        grad_keyvals = lax.dynamic_update_slice_in_dim(grad_keyvals, joined, offset, 1)
        return (grad_query, grad_keyvals)

    kv_init = jnp.zeros(keyvals.shape, jnp.float32)
    initial = (jnp.zeros((groups, length, HEADS, head_size), jnp.float32), kv_init)
    grad_query, grad_keyvals = lax.fori_loop(0, block_count, advance, initial)
    return (grad_query.reshape(groups, length, features), grad_keyvals)


def head_delta(grad_heads_low, outputs_raw):
    return jnp.einsum(
        "sqhd,sqhd->shq", split_heads(grad_heads_low.astype(jnp.float32)), split_heads(outputs_raw)
    )


def body(
    target,
    memory,
    target_seg,
    target_keep,
    memory_seg,
    memory_keep,
    cotangent,
    norm1_gain,
    norm1_bias,
    w_qkv,
    w_out,
    norm2_gain,
    norm2_bias,
    w_cross_q,
    w_cross_kv,
    w_cross_out,
    norm3_gain,
    norm3_bias,
    w_up,
    b_up,
    w_down,
    b_down,
):
    groups, length, features = target.shape
    token_count = groups * length
    target_code = jnp.where(target_keep == 1, target_seg, -1)
    memory_code = jnp.where(memory_keep == 1, memory_seg, -1)
    inputs = target.astype(jnp.float32).reshape(token_count, features)
    normed1, norm1_back = jax.vjp(layer_norm, inputs, norm1_gain, norm1_bias)
    normed1_low = normed1.astype(jnp.bfloat16)
    projected = jnp.dot(normed1_low, w_qkv, preferred_element_type=jnp.float32).astype(jnp.bfloat16)
    projected = projected.reshape(groups, length, 3 * features)
    queries = projected[..., :features]
    keyvals = projected[..., features:]
    self_raw, self_lse = finish_state(
        fold_keys(queries, target_seg)(
            start_state(queries),
            (
                lax.all_gather(keyvals, "blk", axis=1, tiled=True),
                lax.all_gather(target_code, "blk", axis=1, tiled=True),
            ),
            jnp.int32(0),
        )
    )
    self_low = self_raw.astype(jnp.bfloat16).reshape(token_count, features)
    after_self = inputs + jnp.dot(self_low, w_out, preferred_element_type=jnp.float32)
    normed2, norm2_back = jax.vjp(layer_norm, after_self, norm2_gain, norm2_bias)
    normed2_low = normed2.astype(jnp.bfloat16)
    cross_query = jnp.dot(normed2_low, w_cross_q, preferred_element_type=jnp.float32).astype(
        jnp.bfloat16
    )
    cross_query = cross_query.reshape(groups, length, features)
    memory_all, mcodes_all = (
        lax.all_gather(memory, "blk", axis=1, tiled=True),
        lax.all_gather(memory_code, "blk", axis=1, tiled=True),
    )
    memory_keys = jnp.einsum(
        "smd,de->sme", memory_all, w_cross_kv, preferred_element_type=jnp.float32
    ).astype(jnp.bfloat16)
    cross_raw, cross_lse = attend_local(cross_query, target_seg, memory_keys, mcodes_all)
    cross_low = cross_raw.astype(jnp.bfloat16).reshape(token_count, features)
    after_cross = after_self + jnp.dot(cross_low, w_cross_out, preferred_element_type=jnp.float32)
    normed3, norm3_back = jax.vjp(layer_norm, after_cross, norm3_gain, norm3_bias)
    normed3_low = normed3.astype(jnp.bfloat16)
    hidden = jnp.dot(normed3_low, w_up, preferred_element_type=jnp.float32) + b_up
    activated, gelu_back = jax.vjp(jax.nn.gelu, hidden)
    activated_low = activated.astype(jnp.bfloat16)
    block_out = (
        after_cross + jnp.dot(activated_low, w_down, preferred_element_type=jnp.float32) + b_down
    )
    grad_out = cotangent.astype(jnp.float32).reshape(token_count, features)
    grad_branch = grad_out.astype(jnp.bfloat16)
    grad_w_down = jnp.einsum(
        "nf,nd->fd", activated_low, grad_branch, preferred_element_type=jnp.float32
    )
    grad_b_down = jnp.sum(grad_branch.astype(jnp.float32), axis=0)
    (grad_hidden,) = gelu_back(
        jnp.einsum("nd,fd->nf", grad_branch, w_down, preferred_element_type=jnp.float32)
    )
    grad_hidden_low = grad_hidden.astype(jnp.bfloat16)
    grad_w_up = jnp.einsum(
        "nd,nf->df", normed3_low, grad_hidden_low, preferred_element_type=jnp.float32
    )
    grad_b_up = jnp.sum(grad_hidden_low.astype(jnp.float32), axis=0)
    grad_normed3 = jnp.einsum(
        "nf,df->nd", grad_hidden_low, w_up, preferred_element_type=jnp.float32
    )
    grad_cross_side, grad_norm3_gain, grad_norm3_bias = norm3_back(grad_normed3)
    grad_after_cross = grad_out + grad_cross_side
    grad_cross_low = grad_after_cross.astype(jnp.bfloat16)
    grad_w_cross_out = jnp.einsum(
        "nd,ne->de", cross_low, grad_cross_low, preferred_element_type=jnp.float32
    )
    grad_cross_heads = jnp.einsum(
        "ne,de->nd", grad_cross_low, w_cross_out, preferred_element_type=jnp.float32
    ).astype(jnp.bfloat16)
    grad_cross_heads = grad_cross_heads.reshape(groups, length, features)
    cross_delta = head_delta(grad_cross_heads, cross_raw)
    grad_cross_query, grad_memory_part = attend_back(
        cross_query, target_seg, grad_cross_heads, cross_lse, cross_delta, memory_keys, mcodes_all
    )
    grad_memory_keys = lax.psum_scatter(
        grad_memory_part.astype(jnp.bfloat16), "blk", scatter_dimension=1, tiled=True
    )
    grad_w_cross_kv = jnp.einsum(
        "smd,sme->de", memory, grad_memory_keys, preferred_element_type=jnp.float32
    )
    memory_grad = jnp.einsum(
        "sme,de->smd", grad_memory_keys, w_cross_kv, preferred_element_type=jnp.float32
    )
    grad_query_low = grad_cross_query.astype(jnp.bfloat16).reshape(token_count, features)
    grad_w_cross_q = jnp.einsum(
        "nd,ne->de", normed2_low, grad_query_low, preferred_element_type=jnp.float32
    )
    grad_self_side, grad_norm2_gain, grad_norm2_bias = norm2_back(
        jnp.einsum("ne,de->nd", grad_query_low, w_cross_q, preferred_element_type=jnp.float32)
    )
    grad_after_self = grad_after_cross + grad_self_side
    grad_self_low = grad_after_self.astype(jnp.bfloat16)
    grad_w_out = jnp.einsum(
        "nd,ne->de", self_low, grad_self_low, preferred_element_type=jnp.float32
    )
    grad_self_heads = jnp.einsum(
        "ne,de->nd", grad_self_low, w_out, preferred_element_type=jnp.float32
    ).astype(jnp.bfloat16)
    grad_self_heads = grad_self_heads.reshape(groups, length, features)
    self_delta = head_delta(grad_self_heads, self_raw)
    keys_all, codes_all = (
        lax.all_gather(keyvals, "blk", axis=1, tiled=True),
        lax.all_gather(target_code, "blk", axis=1, tiled=True),
    )
    grad_query, grad_keys_part = attend_back(
        queries, target_seg, grad_self_heads, self_lse, self_delta, keys_all, codes_all
    )
    grad_keyvals = lax.psum_scatter(
        grad_keys_part.astype(jnp.bfloat16), "blk", scatter_dimension=1, tiled=True
    ).astype(jnp.float32)
    grad_projected = jnp.concatenate([grad_query, grad_keyvals], axis=-1).astype(jnp.bfloat16)
    grad_projected = grad_projected.reshape(token_count, 3 * features)
    grad_w_qkv = jnp.einsum(
        "nd,ne->de", normed1_low, grad_projected, preferred_element_type=jnp.float32
    )
    grad_input_side, grad_norm1_gain, grad_norm1_bias = norm1_back(
        jnp.einsum("ne,de->nd", grad_projected, w_qkv, preferred_element_type=jnp.float32)
    )
    target_grad = (grad_after_self + grad_input_side).reshape(groups, length, features)
    (
        grad_norm1_gain,
        grad_norm1_bias,
        grad_w_qkv,
        grad_w_out,
        grad_norm2_gain,
        grad_norm2_bias,
        grad_w_cross_q,
        grad_w_cross_kv,
        grad_w_cross_out,
        grad_norm3_gain,
        grad_norm3_bias,
        grad_w_up,
        grad_b_up,
        grad_w_down,
        grad_b_down,
    ) = lax.psum(
        (
            grad_norm1_gain,
            grad_norm1_bias,
            grad_w_qkv,
            grad_w_out,
            grad_norm2_gain,
            grad_norm2_bias,
            grad_w_cross_q,
            grad_w_cross_kv,
            grad_w_cross_out,
            grad_norm3_gain,
            grad_norm3_bias,
            grad_w_up,
            grad_b_up,
            grad_w_down,
            grad_b_down,
        ),
        ("dp", "blk"),
    )
    return (
        block_out.reshape(groups, length, features),
        target_grad,
        memory_grad,
        grad_norm1_gain,
        grad_norm1_bias,
        grad_w_qkv,
        grad_w_out,
        grad_norm2_gain,
        grad_norm2_bias,
        grad_w_cross_q,
        grad_w_cross_kv,
        grad_w_cross_out,
        grad_norm3_gain,
        grad_norm3_bias,
        grad_w_up,
        grad_b_up,
        grad_w_down,
        grad_b_down,
    )


def solution(mesh):
    placed = (
        P("dp", "blk", None),
        P("dp", "blk", None),
        P("dp", "blk"),
        P("dp", "blk"),
        P("dp", "blk"),
        P("dp", "blk"),
        P("dp", "blk", None),
        P(),
        P(),
        P(),
        P(),
        P(),
        P(),
        P(),
        P(),
        P(),
        P(),
        P(),
        P(),
        P(),
        P(),
        P(),
    )
    return jax.shard_map(
        body,
        mesh=mesh,
        in_specs=placed,
        out_specs=(
            P("dp", "blk", None),
            P("dp", "blk", None),
            P("dp", "blk", None),
            P(),
            P(),
            P(),
            P(),
            P(),
            P(),
            P(),
            P(),
            P(),
            P(),
            P(),
            P(),
            P(),
            P(),
            P(),
        ),
        check_vma=False,
    )
```

profile of v0, /device:TPU:0, one launch (start us, length us, event | category | flops | bytes accessed | tf_op | source)
XLA Modules:
  0.0 1627.4 jit_solution(1602484571080416243)
XLA Ops:
  24.9 15.8 all_gather.14
  40.8 14.3 all_gather.16
  59.7 35.2 %all-gather.5.cloned.1.call-done = bf16[4,2048,512]{2,1,0:T(8,128)(2,1)} async-done(((bf16[4,256,512]{2,1,0:T(8,128)(2,1)}), bf16[4,2048,512]{2,1,0:T(8,128)(2,1)}) %all-gather.5.cloned.1.call-update) | async-done | bytes 8388624 | tf_op jit(solution)/shard_map/all_gather | solution.py:207
  94.9 14.9 convolution_convert_fusion
  109.8 21.9 %copy.70 = bf16[4,2048,1024]{1,2,0:T(8,128)(2,1)} copy(bf16[4,2048,1024]{2,1,0:T(8,128)(2,1)} %convolution_convert_fusion) | data formatting | bytes 33554432
  131.7 115.8 %all-gather.3.cloned.1.call-done = bf16[4,2048,1024]{1,2,0:T(8,128)(2,1)} async-done(((bf16[4,256,1024]{1,2,0:T(8,128)(2,1)}), bf16[4,2048,1024]{1,2,0:T(8,128)(2,1)}) %all-gather.3.cloned.1.call-update) | async-done | bytes 16777232 | tf_op jit(solution)/shard_map/all_gather | solution.py:192
  247.5 12.2 fusion.88
  259.7 27.5 %select_reduce_fusion = (f32[4,8,256]{2,1,0:T(8,128)S(1)}, f32[4,8,256,2048]{3,2,1,0:T(8,128)}) fusion(pred[4,256,2048]{2,1,0:T(8,128)(4,1)S(1)} %copy-done.19, bf16[4,256,8,64]{1,3,2,0:T(8,128)(2,1)S(1)} %bitcast.339, bf16[4,2048,8,64]{1,3,2,0:T(8,128)(2,1)} %bitcast.347), kind=kOutput, calls=%fused_computation.64 | convolution fusion | flops 2197807104 | bytes 78675968 | tf_op jit(solution)/shard_map/sqhd,skhd->shqk/dot_general | solution.py:21
  287.2 25.8 %fusion.38 = f32[4,8,256]{2,1,0:T(8,128)S(1)} fusion(f32[4,8,256,2048]{3,2,1,0:T(8,128)} %get-tuple-element.837, f32[4,8,256]{2,1,0:T(8,128)S(1)} %broadcast_maximum_fusion, pred[4,256,2048]{2,1,0:T(8,128)(4,1)} %broadcast_compare_fusion.3), kind=kLoop, calls=%fused_computation.65 | loop fusion | flops 67100672 | bytes 69271552 | tf_op jit(solution)/shard_map/reduce_sum | solution.py:50
  313.7 28.3 %fusion.89 = (bf16[4,256,8,64]{1,3,2,0:T(8,128)(2,1)S(1)}, f32[4,256,8,64]{1,3,2,0:T(8,128)}) fusion(f32[4,256,8]{1,2,0:T(8,128)S(1)} %bitcast_add_fusion.6, bf16[4,2048,8,64]{1,3,2,0:T(8,128)(2,1)} %bitcast.350, f32[4,8,256,2048]{3,2,1,0:T(8,128)} %get-tuple-element.837, f32[4,8,256]{2,1,0:T(8,128)S(1)} %broadcast_maximum_fusion, ...), kind=kOutput, calls=%fused_computation.172 | convolution fusion | flops 2216165376 | bytes 80838656 | tf_op jit(solution)/shard_map/shqk,skhd->sqhd/dot_general | solution.py:51
  351.8 131.6 %while.53 = (s32[]{:T(128)}, f32[4,8,256]{2,1,0:T(8,128)S(1)}, f32[4,8,256]{2,1,0:T(8,128)S(1)}, f32[4,256,8,64]{1,3,2,0:T(8,128)}, s32[4,256]{1,0:T(4,128)S(1)}...) while((s32[]{:T(128)}, f32[4,8,256]{2,1,0:T(8,128)S(1)}, ...), condition=%wide.wide.region_9.10_spmd.clone, body=%wide.wide.region_6.9_spmd.clone.sunk | while | flops 1122025472 | bytes 75002096 | solution.py:83
  364.1 11.1 bitcast_add_fusion.13
  375.3 9.2 fusion.223
  396.5 11.7 bitcast_add_fusion.13
  408.2 9.2 fusion.223
  429.5 11.7 bitcast_add_fusion.13
  441.2 9.2 fusion.223
  462.4 11.7 bitcast_add_fusion.13
  474.2 9.2 fusion.223
  494.7 8.6 convert_reduce_fusion
  528.7 194.8 %while.54 = (s32[]{:T(128)}, f32[4,256,8,64]{1,3,2,0:T(8,128)}, bf16[4,2048,1024]{1,2,0:T(8,128)(2,1)}, bf16[4,2048,1024]{1,2,0:T(8,128)(2,1)}, s32[4,256]{1,0:T...) while((s32[]{:T(128)}, f32[4,256,8,64]{1,3,2,0:T(8,128)}, ...), condition=%wide.wide.region_15.16_spmd.clone, body=%wide.wide.region_14.15_spmd.clone.sunk | while | flops 2738880512 | bytes 148500752 | solution.py:143
  531.7 8.2 fusion.235
  540.4 9.2 fusion.236
  555.7 10.9 fusion.237
  579.9 8.2 fusion.235
  588.5 9.2 fusion.236
  603.8 10.9 fusion.237
  628.6 8.2 fusion.235
  637.3 9.2 fusion.236
  652.6 10.9 fusion.237
  677.4 8.2 fusion.235
  686.0 9.2 fusion.236
  701.3 10.9 fusion.237
  744.4 233.0 %while.52 = (s32[]{:T(128)}, f32[4,256,8,64]{1,3,2,0:T(8,128)}, bf16[4,2048,1024]{2,1,0:T(8,128)(2,1)}, bf16[4,2048,1024]{1,2,0:T(8,128)(2,1)}, s32[4,256]{1,0:T...) while((s32[]{:T(128)}, f32[4,256,8,64]{1,3,2,0:T(8,128)}, ...), condition=%wide.region_19.20_spmd.clone, body=%wide.region_18.19_spmd.clone.sunk | while | flops 2738880512 | bytes 165277968 | solution.py:143
  747.2 8.2 fusion.215
  756.5 9.2 fusion.216
  769.9 10.9 fusion.217
  804.9 8.2 fusion.215
  814.2 9.2 fusion.216
  827.5 10.9 fusion.217
  872.5 9.2 fusion.216
  885.8 10.9 fusion.217
  930.8 9.2 fusion.216
  944.1 10.9 fusion.217
  1001.0 143.0 %reduce-scatter.3.cloned.1.call-done = bf16[4,256,1024]{2,1,0:T(8,128)(2,1)} async-done(((bf16[4,2048,1024]{2,1,0:T(8,128)(2,1)}), bf16[4,256,1024]{2,1,0:T(8,128)(2,1)}) %reduce-scatter.3.cloned.1.call-update) | async-done | bytes 2097168 | tf_op jit(solution)/shard_map/reduce_scatter | solution.py:288
  1149.4 163.5 %reduce-scatter.5.cloned.1.call-done = bf16[4,256,1024]{1,2,0:T(8,128)(2,1)} async-done(((bf16[4,2048,1024]{1,2,0:T(8,128)(2,1)}), bf16[4,256,1024]{1,2,0:T(8,128)(2,1)}) %reduce-scatter.5.cloned.1.call-update) | async-done | bytes 2097168 | tf_op jit(solution)/shard_map/reduce_scatter | solution.py:255
  1329.1 40.4 %all-reduce = (f32[512]{0:T(512)}, f32[512]{0:T(512)}, f32[512]{0:T(512)}, f32[512]{0:T(512)}, f32[512]{0:T(512)}, /*index=5*/f32[512]{0:T(512)}, f32[2048]{0:T(1024)}, f32[512]{0:T(512)}) all-reduce(f32[512]{0:T(512)S(1)} %get-tuple-element.735, f32[512]{0:T(512)S(1)} %get-tuple-element.739, ...), channel_id=1, replica_groups=mesh['dp'=4,'blk'=8] {'dp','blk'}, use_global_device_ids=true, to_apply=%region_25.26 | all-reduce | flops 5632 | bytes 45056 | tf_op jit(solution)/shard_map/psum | solution.py:316
  1376.3 227.7 %all-reduce.4.cloned.1.call-done = (f32[512,1536]{1,0:T(8,128)}, f32[512,512]{1,0:T(8,128)}, f32[512,512]{1,0:T(8,128)}, f32[512,1024]{0,1:T(8,128)}, f32[512,51...) async-done(((f32[512,1536]{1,0:T(8,128)}, f32[512,512]{1,0:T(8,128)}, f32[512,512]{1,0:T(8,128)}, f32[512,1024]{0,1:T(8,128)}, f32[512,512]{1,0:T(8,128)}, ...) | async-done | bytes 16777232 | tf_op jit(solution)/shard_map/psum | solution.py:316
  (437 shorter events, 422.9 us)
Async XLA Ops:
  7.2 481.1 %copy-start = (bf16[512,2048]{1,0:T(8,128)(2,1)S(1)}, bf16[512,2048]{1,0:T(8,128)(2,1)}, u32[]{:S(2)}) copy-start(bf16[512,2048]{1,0:T(8,128)(2,1)} %param.46) | copy-start | bytes 6291460
  7.2 87.6 %all-gather.5.cloned.1.call-start = ((), (), s32[]{:S(2)}) async-start(), calls=%async_computation.3 | async-start | bytes 9437184 | tf_op jit(solution)/shard_map/all_gather | solution.py:207
  8.0 239.5 %all-gather.3.cloned.1.call-start = ((), (), s32[]{:S(2)}) async-start(), calls=%async_computation.2 | async-start | bytes 18874368 | tf_op jit(solution)/shard_map/all_gather | solution.py:192
  20.9 19.9 %copy-start.90 = (s32[4,256]{1,0:T(4,128)S(1)}, s32[4,256]{1,0:T(4,128)}, u32[]{:S(2)}) copy-start(s32[4,256]{1,0:T(4,128)} %param.32) | copy-start | bytes 12292
  20.9 19.9 %copy-start.91 = (s32[4,256]{1,0:T(4,128)S(1)}, s32[4,256]{1,0:T(4,128)}, u32[]{:S(2)}) copy-start(s32[4,256]{1,0:T(4,128)} %param.33) | copy-start | bytes 12292
  20.9 1123.0 %reduce-scatter.3.cloned.1.call-start = ((), (), s32[]{:S(2)}) async-start(), calls=%async_computation.4 | async-start | bytes 18874368 | tf_op jit(solution)/shard_map/reduce_scatter | solution.py:288
  24.9 234.7 %copy-start.4 = (bf16[4,256,512]{1,2,0:T(8,128)(2,1)}, bf16[4,256,512]{1,2,0:T(8,128)(2,1)S(1)}, u32[]{:S(2)}) copy-start(bf16[4,256,512]{1,2,0:T(8,128)(2,1)S(1)} %copy.113) | copy-start | bytes 3145732
  40.8 16.6 %copy-start.60 = (s32[4,2048]{1,0:T(4,128)}, s32[4,2048]{1,0:T(4,128)S(1)}, u32[]{:S(2)}) copy-start(s32[4,2048]{1,0:T(4,128)S(1)} %all_gather.14) | copy-start | bytes 98308
  247.5 12.2 copy-start.19
  487.8 18.9 %copy-start.11 = (f32[1024,512]{1,0:T(8,128)}, f32[1024,512]{1,0:T(8,128)S(1)}, u32[]{:S(2)}) copy-start(f32[1024,512]{1,0:T(8,128)S(1)} %get-tuple-element.843) | copy-start | bytes 6291460
  487.9 18.8 %copy-start.61 = (f32[1024]{0:T(1024)}, f32[1024]{0:T(1024)S(1)}, u32[]{:S(2)}) copy-start(f32[1024]{0:T(1024)S(1)} %broadcast_multiply_fusion) | copy-start | bytes 12292
  488.7 18.1 %copy-start.63 = (f32[1024]{0:T(1024)}, f32[1024]{0:T(1024)S(1)}, u32[]{:S(2)}) copy-start(f32[1024]{0:T(1024)S(1)} %fusion.76) | copy-start | bytes 12292
  488.7 6.1 copy-start.50
  488.7 6.1 copy-start.98
  540.4 9.2 copy-start.25
  549.6 6.1 copy-start.3
  588.5 9.2 copy-start.25
  597.8 6.1 copy-start.3
  637.3 9.2 copy-start.25
  646.5 6.1 copy-start.3
  686.0 9.2 copy-start.25
  695.3 6.1 copy-start.3
  738.3 6.1 copy-start.5
  738.3 6.1 copy-start.79
  756.5 9.2 copy-start.26
  814.2 9.2 copy-start.26
  872.5 9.2 copy-start.26
  930.7 9.2 copy-start.26
  977.4 335.4 %reduce-scatter.5.cloned.1.call-start = ((), (), s32[]{:S(2)}) async-start(), calls=%async_computation.5 | async-start | bytes 18874368 | tf_op jit(solution)/shard_map/reduce_scatter | solution.py:255
  977.9 626.0 %all-reduce.4.cloned.1.call-start = ((), (), s32[]{:S(2)}) async-start(), calls=%async_computation.6 | async-start | bytes 33554432 | tf_op jit(solution)/shard_map/psum | solution.py:316
  989.5 6.8 copy-start.12
  989.5 6.8 copy-start.28
  989.5 6.8 copy-start.62
  989.5 6.8 copy-start.64
  989.5 6.8 copy-start.81
  989.5 6.8 copy-start.87
  996.3 147.7 %copy-start.47 = (bf16[1024,512]{1,0:T(8,128)(2,1)S(1)}, bf16[1024,512]{1,0:T(8,128)(2,1)}, u32[]{:S(2)}) copy-start(bf16[1024,512]{1,0:T(8,128)(2,1)} %reshape.354) | copy-start | bytes 3145732
  1318.7 6.7 copy-start.15
  1318.7 6.7 copy-start.48
  1318.7 6.7 copy-start.68
  1318.7 6.7 copy-start.83
  1318.7 6.7 copy-start.99
  1318.7 6.7 copy-start.101
  1327.5 42.0 %copy-start.34 = (f32[1024,512]{1,0:T(8,128)}, f32[1024,512]{1,0:T(8,128)S(1)}, u32[]{:S(2)}) copy-start(f32[1024,512]{1,0:T(8,128)S(1)} %get-tuple-element.848) | copy-start | bytes 6291460
  1369.5 4.7 copy-start.18
  1369.5 4.8 copy-start.35
  1606.8 4.9 copy-start.57
  1606.8 5.9 copy-start.56
  (78 other events, 166.8 us)
Sparse Core Ops, SparseCore 0:
  9.7 85.1 all-gather.4
  97.0 150.4 all-gather.2
  977.5 166.4 reduce-scatter.2
  1146.2 166.6 reduce-scatter.4
  1320.2 283.6 all-reduce.3
where the time goes:
time: 1630 us
  waiting for transfers between devices  686 us (42%)
  matrix products  533 us (33%)
  local copies, waits for them, and re-layouts  191 us (12%)
  other arithmetic  129 us (8%)
  blocking collectives  70.5 us (4%)
    psum x1, waiting for transfers between devices, body(): lax.psum((grad_norm1_gain, grad_norm1_bias, grad_w_qkv, grad_w_out, grad_...  228 us
    reduce_scatter x1, waiting for transfers between devices, body(): lax.psum_scatter(grad_memory_part.astype(jnp.bfloat16), 'blk', scatter_di...  163 us
    reduce_scatter x1, waiting for transfers between devices, body(): lax.psum_scatter(grad_keys_part.astype(jnp.bfloat16), 'blk', scatter_dime...  143 us
    dot_general x13, matrix products, block_scores(): jnp.einsum('sqhd,skhd->shqk', split_heads(queries), split_heads(keys_now)...  122 us
    all_gather x1, waiting for transfers between devices, body(): lax.all_gather(keyvals, 'blk', axis=1, tiled=True)  116 us
    dot_general x8, matrix products, advance(): jnp.einsum('shqk,sqhd->skhd', probability.astype(jnp.bfloat16), grad_head...  86.9 us
    dot_general x5, matrix products, absorb(): jnp.einsum('shqk,skhd->sqhd', weights.astype(jnp.bfloat16), split_heads(k...  74.6 us
    dot_general x8, matrix products, advance(): jnp.einsum('sqhd,skhd->shqk', grad_heads, split_heads(kv_block[..., featu...  73.7 us
  transfers between devices with their start and end apart: 5, of which 5 were waited for; matrix products, arithmetic and copies ran while one was open for 6% of the time, Pallas kernels for 0%

commit v1 on v0

v1 whole, which is shorter than its diff:
```python
import functools
import math

import jax
import jax.numpy as jnp
from jax import lax
from jax.experimental import pallas as pl
from jax.experimental.pallas import tpu as pltpu
from jax.sharding import PartitionSpec as P

HEADS = 8
NT = (((1,), (1,)), ((), ()))
NN = (((1,), (0,)), ((), ()))
TN = (((0,), (0,)), ((), ()))
f32 = jnp.float32
bf16 = jnp.bfloat16
VMEM = 60 * 1024 * 1024
QUERY_SCALE = 0.125 * math.log2(math.e)
HIDDEN_MASK = -1e30


def dot(left, right, dims=NN):
    return lax.dot_general(left, right, dims, preferred_element_type=f32)


def layer_norm(values, scale_gain, shift_bias):
    centered = values - jnp.mean(values, axis=-1, keepdims=True)
    spread = jnp.mean(centered * centered, axis=-1, keepdims=True)
    return centered * lax.rsqrt(spread + 1e-05) * scale_gain + shift_bias


def forward_kernel(q_ref, k_ref, v_ref, qmask_ref, kmask_ref, o_ref, lse_ref):
    low = lax.broadcasted_iota(jnp.int32, (1, 128), 1) < 64
    q, k, v = q_ref[...], k_ref[...], v_ref[...]
    qmask, kmask = qmask_ref[...], kmask_ref[...]
    outputs = []
    for head in range(2):
        mine = low if head == 0 else ~low
        scores = dot(jnp.where(mine, k, kmask), jnp.where(mine, q, qmask), NT)
        largest = jnp.max(scores, axis=0, keepdims=True)
        weights = jnp.exp2(scores - largest).astype(bf16)
        both = dot(jnp.where(mine, v, jnp.ones_like(v)), weights, TN)
        total = both[64 - head * 64 : 65 - head * 64]
        lse_ref[0, head : head + 1, :] = largest + jnp.log2(total)
        outputs.append(both[head * 64 : head * 64 + 64] / total)
    o_ref[...] = jnp.concatenate(outputs, 0).T.astype(bf16)


def attend(queries, keys, values, qmask, kmask):
    tokens, features = queries.shape
    length = keys.shape[0]
    pairs = features // 128
    of_queries = pl.BlockSpec((tokens, 128), lambda h: (0, h))
    of_keys = pl.BlockSpec((length, 128), lambda h: (0, h))
    return pl.pallas_call(
        forward_kernel,
        grid=(pairs,),
        in_specs=[
            of_queries,
            of_keys,
            of_keys,
            pl.BlockSpec((tokens, 128), lambda h: (0, 0)),
            pl.BlockSpec((length, 128), lambda h: (0, 0)),
        ],
        out_specs=[of_queries, pl.BlockSpec((1, 2, tokens), lambda h: (h, 0, 0))],
        out_shape=[
            jax.ShapeDtypeStruct((tokens, features), bf16),
            jax.ShapeDtypeStruct((pairs, 2, tokens), f32),
        ],
        compiler_params=pltpu.CompilerParams(vmem_limit_bytes=VMEM),
        cost_estimate=pl.CostEstimate(
            flops=HEADS * 4 * tokens * length * 128,
            bytes_accessed=2 * features * (2 * tokens + 2 * length),
            transcendentals=HEADS * tokens * length,
        ),
        name="attend",
    )(queries, keys, values, qmask, kmask)


def backward_kernel(
    chunk, q_ref, k_ref, v_ref, qmask_ref, kmask_ref, do_ref, o_ref, lse_ref, dq_ref, dk_ref, dv_ref
):
    low = lax.broadcasted_iota(jnp.int32, (1, 128), 1) < 64
    q, qmask, grad = q_ref[...], qmask_ref[...], do_ref[...]
    tokens, length = q.shape[0], k_ref.shape[0]
    product = grad.astype(f32) * o_ref[...].astype(f32)
    upper = product.astype(bf16)
    lower = (product - upper.astype(f32)).astype(bf16)
    rows = lax.broadcasted_iota(jnp.int32, (8, 128), 0)
    lanes = lax.broadcasted_iota(jnp.int32, (8, 128), 1)
    pick = jnp.where(rows == lanes // 64, 1.0, 0.0).astype(bf16)
    delta = dot(pick, upper, NT) + dot(pick, lower, NT)
    lse = lse_ref[0]
    zero = jnp.zeros_like(grad)
    q_heads = [jnp.where(low, q, qmask), jnp.where(low, qmask, q)]
    grad_heads = [jnp.where(low, grad, zero), jnp.where(low, zero, grad)]
    dq = [jnp.zeros((64, tokens), f32)] * 2
    for start in range(0, length, chunk):
        part = slice(start, start + chunk)
        k, v, kmask = k_ref[part, :], v_ref[part, :], kmask_ref[part, :]
        dk, dv = [], []
        for head in range(2):
            k_head = jnp.where(low, k, kmask) if head == 0 else jnp.where(low, kmask, k)
            weights = jnp.exp2(dot(k_head, q_heads[head], NT) - lse[head : head + 1, :])
            grad_weights = dot(v, grad_heads[head], NT)
            grad_scores = (weights * (grad_weights - delta[head : head + 1, :])).astype(bf16)
            dv.append(dot(weights.astype(bf16), grad))
            dk.append(dot(grad_scores, q))
            dq[head] = dq[head] + dot(k, grad_scores, TN)[head * 64 : head * 64 + 64]
        dk_ref[part, :] = (jnp.where(low, dk[0], dk[1]) * math.log(2.0)).astype(bf16)
        dv_ref[part, :] = jnp.where(low, dv[0], dv[1]).astype(bf16)
    dq_ref[...] = (jnp.concatenate(dq, 0).T * 0.125).astype(bf16)


def attend_back(queries, keys, values, qmask, kmask, grad, outputs, lse):
    tokens, features = queries.shape
    length = keys.shape[0]
    pairs = features // 128
    of_queries = pl.BlockSpec((tokens, 128), lambda h: (0, h))
    of_keys = pl.BlockSpec((length, 128), lambda h: (0, h))
    return pl.pallas_call(
        functools.partial(backward_kernel, min(1024, length)),
        grid=(pairs,),
        in_specs=[
            of_queries,
            of_keys,
            of_keys,
            pl.BlockSpec((tokens, 128), lambda h: (0, 0)),
            pl.BlockSpec((length, 128), lambda h: (0, 0)),
            of_queries,
            of_queries,
            pl.BlockSpec((1, 2, tokens), lambda h: (h, 0, 0)),
        ],
        out_specs=[of_queries, of_keys, of_keys],
        out_shape=[
            jax.ShapeDtypeStruct((tokens, features), bf16),
            jax.ShapeDtypeStruct((length, features), bf16),
            jax.ShapeDtypeStruct((length, features), bf16),
        ],
        compiler_params=pltpu.CompilerParams(vmem_limit_bytes=VMEM),
        cost_estimate=pl.CostEstimate(
            flops=HEADS * 10 * tokens * length * 128,
            bytes_accessed=2 * features * (4 * tokens + 4 * length),
            transcendentals=HEADS * tokens * length,
        ),
        name="attend_back",
    )(queries, keys, values, qmask, kmask, grad, outputs, lse)


class Layout:
    def __init__(self, rows, blocks):
        self.rows = rows
        self.share = blocks // rows
        index = lax.axis_index("blk")
        self.row = index // self.share

    def shift_rows(self, step):
        rows, share = self.rows, self.share
        return [
            (a * share + b, ((a + step) % rows) * share + b) for a in range(rows) for b in range(share)
        ]

    def shift_share(self, step):
        rows, share = self.rows, self.share
        return [
            (a * share + b, a * share + (b + step) % share) for a in range(rows) for b in range(share)
        ]

    def gather_row(self, values):
        parts = []
        for step in range(self.rows):
            wanted = lax.rem(self.row + step, self.rows)
            part = lax.dynamic_index_in_dim(values, wanted, 0, keepdims=False)
            if step:
                part = lax.ppermute(part, "blk", self.shift_rows(step))
            parts.append(part)
        return jnp.concatenate(parts, 0)

    def return_row(self, values):
        tokens, features = values.shape
        parts = values.reshape(self.rows, tokens // self.rows, features)
        result = jnp.zeros(parts.shape, f32)
        for step in range(self.rows):
            part = parts[step]
            if step:
                part = lax.ppermute(part.astype(bf16), "blk", self.shift_rows(self.rows - step))
            home = lax.rem(self.row + step, self.rows)
            result = lax.dynamic_update_index_in_dim(result, part.astype(f32), home, 0)
        return result

    def gather_share(self, values):
        parts = [values]
        for step in range(1, self.share):
            parts.append(lax.ppermute(values, "blk", self.shift_share(step)))
        return jnp.concatenate(parts, 0)

    def sum_share(self, values):
        tokens = values.shape[0] // self.share
        total = values[:tokens].astype(f32)
        for step in range(1, self.share):
            part = values[step * tokens : (step + 1) * tokens]
            total = total + lax.ppermute(part, "blk", self.shift_share(self.share - step)).astype(f32)
        return total.astype(bf16)


def query_mask(segments):
    lanes = lax.broadcasted_iota(jnp.int32, (1, 128), 1) % 64
    return jnp.where(segments[:, None] == lanes, 1.0, 0.0).astype(bf16)


def key_mask(codes):
    lanes = lax.broadcasted_iota(jnp.int32, (1, 128), 1) % 64
    return jnp.where((codes[:, None] != lanes) & (lanes < 3), HIDDEN_MASK, 0.0).astype(bf16)


def body(
    blocks,
    target,
    memory,
    target_seg,
    target_keep,
    memory_seg,
    memory_keep,
    cotangent,
    norm1_gain,
    norm1_bias,
    w_qkv,
    w_out,
    norm2_gain,
    norm2_bias,
    w_cross_q,
    w_cross_kv,
    w_cross_out,
    norm3_gain,
    norm3_bias,
    w_up,
    b_up,
    w_down,
    b_down,
):
    rows, length, features = target.shape
    layout = Layout(rows, blocks)
    packed = jnp.stack(
        [target_seg + 4 * (target_keep != 1), memory_seg + 4 * (memory_keep != 1)], axis=-1
    )
    target_row = layout.gather_row(target)
    packed_row = layout.gather_row(packed)
    packed_all = layout.gather_share(packed_row)
    memory_row = layout.gather_row(memory)
    grad_branch = layout.gather_row(cotangent)
    qmask = query_mask(packed_row[:, 0] % 4)
    self_kmask = key_mask(packed_all[:, 0])
    cross_kmask = key_mask(packed_all[:, 1])

    inputs = target_row.astype(f32)
    normed1, norm1_back = jax.vjp(layer_norm, inputs, norm1_gain, norm1_bias)
    normed1_low = normed1.astype(bf16)
    keyvals = dot(normed1_low, w_qkv[:, features:]).astype(bf16)
    keyvals = layout.gather_share(keyvals)
    queries = (dot(normed1_low, w_qkv[:, :features]) * QUERY_SCALE).astype(bf16)
    keys, values = keyvals[:, :features], keyvals[:, features:]
    memory_kv = layout.gather_share(dot(memory_row, w_cross_kv).astype(bf16))
    memory_keys, memory_values = memory_kv[:, :features], memory_kv[:, features:]

    self_low, self_lse = attend(queries, keys, values, qmask, self_kmask)
    after_self = inputs + dot(self_low, w_out)
    normed2, norm2_back = jax.vjp(layer_norm, after_self, norm2_gain, norm2_bias)
    normed2_low = normed2.astype(bf16)
    cross_query = (dot(normed2_low, w_cross_q) * QUERY_SCALE).astype(bf16)
    cross_low, cross_lse = attend(cross_query, memory_keys, memory_values, qmask, cross_kmask)
    after_cross = after_self + dot(cross_low, w_cross_out)
    normed3, norm3_back = jax.vjp(layer_norm, after_cross, norm3_gain, norm3_bias)
    normed3_low = normed3.astype(bf16)
    hidden = dot(normed3_low, w_up) + b_up
    activated, gelu_back = jax.vjp(jax.nn.gelu, hidden)
    activated_low = activated.astype(bf16)
    block_out = layout.return_row(after_cross + dot(activated_low, w_down) + b_down)

    grad_out = grad_branch.astype(f32)
    grad_w_down = dot(activated_low, grad_branch, TN)
    grad_b_down = jnp.sum(grad_out, axis=0)
    (grad_hidden,) = gelu_back(dot(grad_branch, w_down, NT))
    grad_hidden_low = grad_hidden.astype(bf16)
    grad_w_up = dot(normed3_low, grad_hidden_low, TN)
    grad_b_up = jnp.sum(grad_hidden_low.astype(f32), axis=0)
    grad_cross_side, grad_norm3_gain, grad_norm3_bias = norm3_back(dot(grad_hidden_low, w_up, NT))
    grad_after_cross = grad_out + grad_cross_side
    grad_cross_low = grad_after_cross.astype(bf16)
    grad_w_cross_out = dot(cross_low, grad_cross_low, TN)
    grad_cross_heads = dot(grad_cross_low, w_cross_out, NT).astype(bf16)

    grad_query_low, grad_mkeys, grad_mvalues = attend_back(
        cross_query, memory_keys, memory_values, qmask, cross_kmask, grad_cross_heads, cross_low, cross_lse
    )
    grad_memory_kv = layout.sum_share(jnp.concatenate([grad_mkeys, grad_mvalues], axis=1))
    grad_w_cross_kv = dot(memory_row, grad_memory_kv, TN)
    memory_grad = layout.return_row(dot(grad_memory_kv, w_cross_kv, NT))
    grad_w_cross_q = dot(normed2_low, grad_query_low, TN)
    grad_self_side, grad_norm2_gain, grad_norm2_bias = norm2_back(dot(grad_query_low, w_cross_q, NT))
    grad_after_self = grad_after_cross + grad_self_side
    grad_self_low = grad_after_self.astype(bf16)
    grad_w_out = dot(self_low, grad_self_low, TN)
    grad_self_heads = dot(grad_self_low, w_out, NT).astype(bf16)

    grad_query, grad_keys, grad_values = attend_back(
        queries, keys, values, qmask, self_kmask, grad_self_heads, self_low, self_lse
    )
    grad_keyvals = layout.sum_share(jnp.concatenate([grad_keys, grad_values], axis=1))
    grad_projected = jnp.concatenate([grad_query, grad_keyvals], axis=-1)
    grad_w_qkv = dot(normed1_low, grad_projected, TN)
    grad_input_side, grad_norm1_gain, grad_norm1_bias = norm1_back(dot(grad_projected, w_qkv, NT))
    target_grad = layout.return_row(grad_after_self + grad_input_side)

    everywhere = ("dp", "blk")

    def total_low(*grads):
        sums = lax.psum(tuple(grad.astype(bf16) for grad in grads), everywhere)
        return [grad.astype(f32) for grad in sums]

    grad_w_down, grad_w_up = total_low(grad_w_down, grad_w_up)
    (grad_w_cross_out, grad_w_cross_q, grad_w_cross_kv, grad_w_out, grad_w_qkv) = total_low(
        grad_w_cross_out, grad_w_cross_q, grad_w_cross_kv, grad_w_out, grad_w_qkv
    )
    (
        grad_norm1_gain,
        grad_norm1_bias,
        grad_norm2_gain,
        grad_norm2_bias,
        grad_norm3_gain,
        grad_norm3_bias,
        grad_b_up,
        grad_b_down,
    ) = lax.psum(
        (
            grad_norm1_gain,
            grad_norm1_bias,
            grad_norm2_gain,
            grad_norm2_bias,
            grad_norm3_gain,
            grad_norm3_bias,
            grad_b_up,
            grad_b_down,
        ),
        everywhere,
    )
    return (
        block_out,
        target_grad,
        memory_grad,
        grad_norm1_gain,
        grad_norm1_bias,
        grad_w_qkv,
        grad_w_out,
        grad_norm2_gain,
        grad_norm2_bias,
        grad_w_cross_q,
        grad_w_cross_kv,
        grad_w_cross_out,
        grad_norm3_gain,
        grad_norm3_bias,
        grad_w_up,
        grad_b_up,
        grad_w_down,
        grad_b_down,
    )


def solution(mesh):
    token = P("dp", "blk", None)
    code = P("dp", "blk")
    return jax.shard_map(
        functools.partial(body, mesh.shape["blk"]),
        mesh=mesh,
        in_specs=(token, token, code, code, code, code, token) + (P(),) * 15,
        out_specs=(token, token, token) + (P(),) * 15,
        check_vma=False,
    )
```

time: 1630 us -> 598 us (0.37)
  waiting for transfers between devices: 686 us -> 153 us
  matrix products: 533 us -> 73.2 us
  Pallas kernels: 0 us -> 137 us
  local copies, waits for them, and re-layouts: 191 us -> 63.4 us
  other arithmetic: 129 us -> 54 us
  starting transfers between devices: 0.2 us -> 47.7 us
  blocking collectives: 70.5 us -> 48.7 us
    dot_general x71 -> x22, matrix products: 533 us -> 73.2 us  [dot(): return lax.dot_general(left, right, dims, preferred_element_type=f32)]
    reduce_scatter x2 -> x0, waiting for transfers between devices: 306 us -> none  [the longest x1 163 us: body(): lax.psum_scatter(grad_memory_part.astype(jnp.bfloat16), 'blk', scatter_di...]
    all_gather x2 -> x0, waiting for transfers between devices: 151 us -> none  [the longest x1 116 us: body(): lax.all_gather(keyvals, 'blk', axis=1, tiled=True)]
    pallas_call x0 -> x4, Pallas kernels: none -> 137 us  [the longest x2 88.3 us: attend_back(): pl.pallas_call(functools.partial(backward_kernel, min(1024, length)), gri...]
    psum x1, waiting for transfers between devices: 228 us -> 122 us  [total_low(): sums = lax.psum(tuple((grad.astype(bf16) for grad in grads)), everywhere)]
    reduce_sum x6 -> x1, other arithmetic: 62.9 us -> 2.16 us  [body(): grad_b_down = jnp.sum(grad_out, axis=0)]
    unnamed x221 -> x184, local copies, waits for them, and re-layouts: 64.1 us -> 12.7 us
    ppermute x0 -> x26, starting transfers between devices: none -> 47.7 us  [the longest x12 37.7 us: gather_row(): part = lax.ppermute(part, 'blk', self.shift_rows(step))]
  transfers between devices with their start and end apart: 5 -> 27, of which waited for: 5 -> 4; matrix products, arithmetic and copies ran while one was open for 6% -> 19% of each run, Pallas kernels for 0% -> 16%
where the time goes in v1:
time: 598 us; the launch traced here: 592 us
  waiting for transfers between devices  153 us (26%)
  Pallas kernels  137 us (23%)
  matrix products  73.2 us (12%)
  local copies, waits for them, and re-layouts  63.4 us (11%)
  other arithmetic  54 us (9%)
  blocking collectives  48.7 us (8%)
  starting transfers between devices  47.7 us (8%)
  between operations  15.5 us (3%)
    psum x1, waiting for transfers between devices, total_low(): sums = lax.psum(tuple((grad.astype(bf16) for grad in grads)), everywhere)  122 us
    pallas_call x2, Pallas kernels, attend_back(): pl.pallas_call(functools.partial(backward_kernel, min(1024, length)), gri...  88.3 us
    dot_general x22, matrix products, dot(): return lax.dot_general(left, right, dims, preferred_element_type=f32)  73.2 us
    psum x1, blocking collectives, body(): lax.psum((grad_norm1_gain, grad_norm1_bias, grad_norm2_gain, grad_norm2_b...  48.7 us
    pallas_call x2, Pallas kernels, attend(): pl.pallas_call(forward_kernel, grid=(pairs,), in_specs=[of_queries, of_ke...  48.6 us
    ppermute x12, starting transfers between devices, gather_row(): part = lax.ppermute(part, 'blk', self.shift_rows(step))  37.7 us
    ppermute x9, waiting for transfers between devices, return_row(): lax.ppermute(part.astype(bf16), 'blk', self.shift_rows(self.rows - step))  23.4 us
    convert_element_type x7, other arithmetic, total_low(): return [grad.astype(f32) for grad in sums]  13.8 us
  transfers between devices with their start and end apart: 27, of which 4 were waited for; matrix products, arithmetic and copies ran while one was open for 19% of the time, Pallas kernels for 16%

profile of v1, /device:TPU:0, one launch (start us, length us, event | category | flops | bytes accessed | tf_op | source)
XLA Modules:
  0.0 592.2 jit_solution(7492800842233082330)
XLA Ops:
  7.4 2.3 dynamic-slice_bitcast_fusion.3
  9.7 5.0 collective-permute-start.10
  14.9 4.3 collective-permute-start.5
  29.9 2.1 collective-permute-start
  31.9 2.4 collective-permute-start.2
  34.4 6.9 %collective-permute-done = bf16[256,512]{0,1:T(8,128)(2,1)S(1)} collective-permute-done((bf16[256,512]{0,1:T(8,128)(2,1)}, bf16[256,512]{0,1:T(8,128)(2,1)S(1)}, u32[]{:S(2)}, u32[]{:S(2)}) %collective-permute-start) | collective-permute-done | bytes 262176 | tf_op jit(solution)/shard_map/ppermute | solution.py:175
  41.3 13.7 %collective-permute-start.9 = (bf16[256,512]{1,0:T(8,128)(2,1)}, bf16[256,512]{1,0:T(8,128)(2,1)S(1)}, u32[]{:S(2)}, u32[]{:S(2)}) collective-permute-start(bf16[256,512]{1,0:T(8,128)(2,1)} %get-tuple-element.85), channel_id=1, source_target_pairs={{0,4},{1,5},{2,6},{3,7},{4,0},{5,1},{6,2},{7,3},{8,12},{9,13},{10,... | collective-permute-start | bytes 786440 | tf_op jit(solution)/shard_map/ppermute | solution.py:175
  58.5 6.6 %collective-permute-start.15 = (bf16[256,512]{0,1:T(8,128)(2,1)}, bf16[256,512]{0,1:T(8,128)(2,1)S(1)}, u32[]{:S(2)}, u32[]{:S(2)}) collective-permute-start(bf16[256,512]{0,1:T(8,128)(2,1)} %bitcast.18), channel_id=1, source_target_pairs={{0,2},{1,3},{2,4},{3,5},{4,6},{5,7},{6,0},{7,1},{8,10},{9,11},{10,... | collective-permute-start | bytes 786440 | tf_op jit(solution)/shard_map/ppermute | solution.py:175
  65.1 2.3 select_convert_fusion
  67.5 3.3 collective-permute-start.16
  71.0 3.7 convolution_convert_fusion.3
  76.5 2.3 pad_maximum_fusion.2
  78.8 24.2 %attend.2 = (bf16[1024,512]{1,0:T(8,128)(2,1)}, f32[4,2,1024]{2,1,0:T(2,128)}) custom-call(bf16[1024,512]{1,0:T(8,128)(2,1)} %multiply_convert_fusion.2.q_ref, bf16[2048,512]{1,0:T(8,128)(2,1)} %get-tuple-element.66.k_ref, bf16[2048,512]{1,0:T(8,128)(2,1)} %get-tuple-element.65.v_ref, bf16[1024,128]{1,0:T(8,128)(2,1)} %select_convert_fusion.2.qmask_ref, ...), custom_call_target="tpu_custom_call" | custom-call | flops 8589934592 | bytes 6291456 | tf_op jit(solution)/shard_map/attend/pallas_call | solution.py:55
  103.0 2.1 fusion.52
  108.5 3.7 pad_maximum_fusion.1
  112.2 24.5 %attend.3 = (bf16[1024,512]{1,0:T(8,128)(2,1)}, f32[4,2,1024]{2,1,0:T(2,128)}) custom-call(bf16[1024,512]{1,0:T(8,128)(2,1)} %multiply_convert_fusion.1.q_ref, bf16[2048,512]{1,0:T(8,128)(2,1)} %get-tuple-element.64.k_ref, bf16[2048,512]{1,0:T(8,128)(2,1)} %get-tuple-element.63.v_ref, bf16[1024,128]{1,0:T(8,128)(2,1)} %select_convert_fusion.2.qmask_ref, ...), custom_call_target="tpu_custom_call" | custom-call | flops 8589934592 | bytes 6291456 | tf_op jit(solution)/shard_map/attend/pallas_call | solution.py:55
  136.7 2.7 fusion.53
  141.8 2.6 fusion.42
  144.5 8.5 %convert_reduce_fusion = (f32[2048]{0:T(1024)S(1)}, bf16[1024,2048]{1,0:T(8,128)(2,1)S(1)}) fusion(f32[1024,2048]{1,0:T(8,128)S(1)} %fusion.42, f32[2048]{0:T(1024)S(1)} %copy-done.74, bf16[2048,512]{1,0:T(8,128)(2,1)S(1)} %copy-done, bf16[256,512]{0,1:T(8,128)(2,1)} %collective-permute-done.17, bf16[256,512]{0,1:T(8,128)(2,1)S(1)} %collective-permute-done.16, ...), kind=kOutput, calls=%fused_computation.9 | convolution fusion | flops 2199910400 | bytes 15745024 | tf_op jit(solution)/shard_map/dot_general | solution.py:23
  153.0 3.7 fusion.58
  156.6 2.9 copy.53
  159.6 3.0 multiply_reduce_fusion
  167.1 44.1 %attend_back.2 = (bf16[1024,512]{1,0:T(8,128)(2,1)}, bf16[2048,512]{1,0:T(8,128)(2,1)}, bf16[2048,512]{1,0:T(8,128)(2,1)}) custom-call(bf16[1024,512]{1,0:T(8,128)(2,1)} %multiply_convert_fusion.1.q_ref, bf16[2048,512]{1,0:T(8,128)(2,1)} %get-tuple-element.64.k_ref, bf16[2048,512]{1,0:T(8,128)(2,1)} %get-tuple-element.63.v_ref, ...), custom_call_target="tpu_custom_call" | custom-call | flops 21474836480 | bytes 12582912 | tf_op jit(solution)/shard_map/attend_back/pallas_call | solution.py:121
  211.2 3.6 fusion.57
  217.9 2.9 copy.54
  220.8 2.7 multiply_reduce_fusion.2
  225.8 2.2 convert_reduce_fusion.2
  236.6 44.3 %attend_back.3 = (bf16[1024,512]{1,0:T(8,128)(2,1)}, bf16[2048,512]{1,0:T(8,128)(2,1)}, bf16[2048,512]{1,0:T(8,128)(2,1)}) custom-call(bf16[1024,512]{1,0:T(8,128)(2,1)} %multiply_convert_fusion.2.q_ref, bf16[2048,512]{1,0:T(8,128)(2,1)} %get-tuple-element.66.k_ref, bf16[2048,512]{1,0:T(8,128)(2,1)} %get-tuple-element.65.v_ref, ...), custom_call_target="tpu_custom_call" | custom-call | flops 21474836480 | bytes 12582912 | tf_op jit(solution)/shard_map/attend_back/pallas_call | solution.py:121
  286.7 7.0 %fusion.54 = (bf16[1024,512]{0,1:T(8,128)(2,1)S(1)}, f32[1024,512]{0,1:T(8,128)S(1)}) fusion(f32[512]{0:T(512)S(1)} %copy-done.76, f32[1024,512]{0,1:T(8,128)S(1)} %copy-done.9, bf16[2048,512]{1,0:T(8,128)(2,1)S(1)} %copy-done, f32[1024,2048]{1,0:T(8,128)} %copy-done.80, f32[2048]{0:T(1024)S(1)} %copy-done.74), kind=kOutput, calls=%fused_computation.176 | convolution fusion | flops 2170028032 | bytes 15738880 | tf_op jit(solution)/shard_map/dot_general | solution.py:23
  296.3 6.7 %convolution_convert_fusion = bf16[2048,512]{1,0:T(8,128)(2,1)} fusion(bf16[256,512]{0,1:T(8,128)(2,1)} %collective-permute-done.17, bf16[256,512]{0,1:T(8,128)(2,1)S(1)} %collective-permute-done.16, bf16[256,512]{0,1:T(8,128)(2,1)S(1)} %collective-permute-done.15, bf16[256,512]{0,1:T(8,128)(2,1)S(1)} %bitcast.107, f32[1024,2048]{1,0:T(8,128)S(1)} %bitcast.119, ...), kind=kOutput, calls=%fused_computation.28 | convolution fusion | flops 2173698048 | bytes 11542528 | tf_op jit(solution)/shard_map/dot_general | solution.py:23
  303.0 3.8 convolution_convert_fusion.1
  312.7 15.3 %collective-permute-done.13 = bf16[256,512]{0,1:T(8,128)(2,1)} collective-permute-done((bf16[256,512]{0,1:T(8,128)(2,1)}, bf16[256,512]{0,1:T(8,128)(2,1)}, u32[]{:S(2)}, u32[]{:S(2)}) %collective-permute-start.13) | collective-permute-done | bytes 262176 | tf_op jit(solution)/shard_map/ppermute | solution.py:186
  336.4 3.3 add_convert_fusion.1
  339.8 3.1 fusion.56
  343.0 3.0 copy.55
  346.0 5.0 fusion.55
  352.0 2.3 collective-permute-start.25
  354.3 4.1 convolution_convert_fusion.5
  358.5 3.1 convolution_convert_fusion.2
  361.6 2.1 fusion.17
  367.9 2.2 copy.56
  370.9 2.4 collective-permute-start.19
  379.8 48.7 %all-reduce = (f32[512]{0:T(512)}, f32[512]{0:T(512)}, f32[512]{0:T(512)}, f32[512]{0:T(512)}, f32[512]{0:T(512)}, /*index=5*/f32[512]{0:T(512)}, f32[2048]{0:T(1024)}, f32[512]{0:T(512)}) all-reduce(f32[512]{0:T(512)S(1)} %get-tuple-element.42, f32[512]{0:T(512)S(1)} %get-tuple-element.106, ...), channel_id=1, replica_groups=mesh['dp'=4,'blk'=8] {'dp','blk'}, use_global_device_ids=true, to_apply=%region_13.14 | all-reduce | flops 5632 | bytes 45056 | tf_op jit(solution)/shard_map/psum | solution.py:333
  430.7 8.0 %collective-permute-done.21 = bf16[256,512]{0,1:T(8,128)(2,1)S(1)} collective-permute-done((bf16[256,512]{0,1:T(8,128)(2,1)}, bf16[256,512]{0,1:T(8,128)(2,1)S(1)}, u32[]{:S(2)}, u32[]{:S(2)}) %collective-permute-start.21) | collective-permute-done | bytes 262176 | tf_op jit(solution)/shard_map/ppermute | solution.py:186
  448.9 122.4 %all-reduce.4.cloned.1.call-done = (bf16[512,1536]{1,0:T(8,128)(2,1)}, bf16[512,512]{1,0:T(8,128)(2,1)}, bf16[512,512]{1,0:T(8,128)(2,1)}, bf16[512,1024]{1,0:T(...) async-done(((bf16[512,1536]{1,0:T(8,128)(2,1)}, bf16[512,512]{1,0:T(8,128)(2,1)}, bf16[512,512]{1,0:T(8,128)(2,1)}, ...) | async-done | bytes 8388624 | tf_op jit(solution)/shard_map/psum | solution.py:317
  571.2 4.3 convert_element_type.172
  575.5 2.6 convert_element_type.175
  578.1 2.1 convert_element_type.162
  (315 shorter events, 92.6 us)
Async XLA Ops:
  7.2 137.3 %copy-start = (bf16[2048,512]{1,0:T(8,128)(2,1)S(1)}, bf16[2048,512]{1,0:T(8,128)(2,1)}, u32[]{:S(2)}) copy-start(bf16[2048,512]{1,0:T(8,128)(2,1)} %param.42) | copy-start | bytes 6291460
  7.2 12.0 %copy-start.39 = (bf16[4,256,512]{2,1,0:T(8,128)(2,1)S(1)}, bf16[4,256,512]{2,1,0:T(8,128)(2,1)}, u32[]{:S(2)}) copy-start(bf16[4,256,512]{2,1,0:T(8,128)(2,1)} %param.28) | copy-start | bytes 3145732
  7.3 564.0 %all-reduce.4.cloned.1.call-start = ((), (), s32[]{:S(2)}) async-start(), calls=%async_computation | async-start | bytes 16777216 | tf_op jit(solution)/shard_map/psum | solution.py:317
  7.4 11.9 %copy-start.40 = (bf16[4,256,512]{2,1,0:T(8,128)(2,1)S(1)}, bf16[4,256,512]{2,1,0:T(8,128)(2,1)}, u32[]{:S(2)}) copy-start(bf16[4,256,512]{2,1,0:T(8,128)(2,1)} %param.22) | copy-start | bytes 3145732
  9.7 57.8 %collective-permute-start.10 = (bf16[256,512]{1,0:T(8,128)(2,1)}, bf16[256,512]{1,0:T(8,128)(2,1)}, u32[]{:S(2)}, u32[]{:S(2)}) collective-permute-start(bf16[256,512]{1,0:T(8,128)(2,1)} %get-tuple-element.84), channel_id=1, source_target_pairs={{0,6},{1,7},{2,0},{3,1},{4,2},{5,3},{6,4},{7,5},{8,14},{9,15},{10,... | collective-permute-start | bytes 786440 | tf_op jit(solution)/shard_map/ppermute | solution.py:175
  14.8 56.0 %collective-permute-start.8 = (bf16[256,512]{1,0:T(8,128)(2,1)}, bf16[256,512]{1,0:T(8,128)(2,1)}, u32[]{:S(2)}, u32[]{:S(2)}) collective-permute-start(bf16[256,512]{1,0:T(8,128)(2,1)} %get-tuple-element.83), channel_id=1, source_target_pairs={{0,2},{1,3},{2,4},{3,5},{4,6},{5,7},{6,0},{7,1},{8,10},{9,11},{10,... | collective-permute-start | bytes 786440 | tf_op jit(solution)/shard_map/ppermute | solution.py:175
  14.8 15.0 %collective-permute-start.4 = (s32[256,2]{0,1:T(2,128)S(1)}, s32[256,2]{0,1:T(2,128)S(1)}, u32[]{:S(2)}, u32[]{:S(2)}) collective-permute-start(s32[256,2]{0,1:T(2,128)S(1)} %bitcast.117), channel_id=1, source_target_pairs={{0,2},{1,3},{2,4},{3,5},{4,6},{5,7},{6,0},{7,1},{8,10},{9,11},{10,... | collective-permute-start | bytes 6152 | tf_op jit(solution)/shard_map/ppermute | solution.py:175
  14.9 17.0 %collective-permute-start.5 = (s32[256,2]{0,1:T(2,128)S(1)}, s32[256,2]{0,1:T(2,128)S(1)}, u32[]{:S(2)}, u32[]{:S(2)}) collective-permute-start(s32[256,2]{0,1:T(2,128)S(1)} %bitcast.116), channel_id=1, source_target_pairs={{0,4},{1,5},{2,6},{3,7},{4,0},{5,1},{6,2},{7,3},{8,12},{9,13},{10,... | collective-permute-start | bytes 6152 | tf_op jit(solution)/shard_map/ppermute | solution.py:175
  19.3 12.7 %collective-permute-start.6 = (s32[256,2]{0,1:T(2,128)S(1)}, s32[256,2]{0,1:T(2,128)S(1)}, u32[]{:S(2)}, u32[]{:S(2)}) collective-permute-start(s32[256,2]{0,1:T(2,128)S(1)} %bitcast.115), channel_id=1, source_target_pairs={{0,6},{1,7},{2,0},{3,1},{4,2},{5,3},{6,4},{7,5},{8,14},{9,15},{10,... | collective-permute-start | bytes 6152 | tf_op jit(solution)/shard_map/ppermute | solution.py:175
  27.1 75.9 %copy-start.15 = (bf16[1,256,512]{1,2,0:T(8,128)(2,1)}, bf16[1,256,512]{1,2,0:T(8,128)(2,1)S(1)}, u32[]{:S(2)}) copy-start(bf16[1,256,512]{1,2,0:T(8,128)(2,1)S(1)} %copy.40) | copy-start | bytes 786436
  27.1 28.4 %copy-start.59 = (f32[512]{0:T(512)S(1)}, f32[512]{0:T(512)}, u32[]{:S(2)}) copy-start(f32[512]{0:T(512)} %param.29) | copy-start | bytes 6148
  27.1 28.4 %copy-start.78 = (f32[512]{0:T(512)S(1)}, f32[512]{0:T(512)}, u32[]{:S(2)}) copy-start(f32[512]{0:T(512)} %param.30) | copy-start | bytes 6148
  29.8 25.7 %copy-start.68 = (bf16[512,1536]{1,0:T(8,128)(2,1)S(1)}, bf16[512,1536]{1,0:T(8,128)(2,1)}, u32[]{:S(2)}) copy-start(bf16[512,1536]{1,0:T(8,128)(2,1)} %param.31) | copy-start | bytes 4718596
  29.9 11.4 %collective-permute-start = (bf16[256,512]{0,1:T(8,128)(2,1)}, bf16[256,512]{0,1:T(8,128)(2,1)S(1)}, u32[]{:S(2)}, u32[]{:S(2)}) collective-permute-start(bf16[256,512]{0,1:T(8,128)(2,1)} %bitcast.110), channel_id=1, source_target_pairs={{0,2},{1,3},{2,4},{3,5},{4,6},{5,7},{6,0},{7,1},{8,10},{9,11},{10,... | collective-permute-start | bytes 786440 | tf_op jit(solution)/shard_map/ppermute | solution.py:175
  31.9 23.0 %collective-permute-start.1 = (bf16[256,512]{0,1:T(8,128)(2,1)}, bf16[256,512]{0,1:T(8,128)(2,1)S(1)}, u32[]{:S(2)}, u32[]{:S(2)}) collective-permute-start(bf16[256,512]{0,1:T(8,128)(2,1)} %bitcast.109), channel_id=1, source_target_pairs={{0,4},{1,5},{2,6},{3,7},{4,0},{5,1},{6,2},{7,3},{8,12},{9,13},{10,... | collective-permute-start | bytes 786440 | tf_op jit(solution)/shard_map/ppermute | solution.py:175
  31.9 23.0 %collective-permute-start.2 = (bf16[256,512]{0,1:T(8,128)(2,1)}, bf16[256,512]{0,1:T(8,128)(2,1)S(1)}, u32[]{:S(2)}, u32[]{:S(2)}) collective-permute-start(bf16[256,512]{0,1:T(8,128)(2,1)} %bitcast.108), channel_id=1, source_target_pairs={{0,6},{1,7},{2,0},{3,1},{4,2},{5,3},{6,4},{7,5},{8,14},{9,15},{10,... | collective-permute-start | bytes 786440 | tf_op jit(solution)/shard_map/ppermute | solution.py:175
  41.3 61.7 %copy-start.17 = (bf16[256,512]{0,1:T(8,128)(2,1)}, bf16[256,512]{0,1:T(8,128)(2,1)S(1)}, u32[]{:S(2)}) copy-start(bf16[256,512]{0,1:T(8,128)(2,1)S(1)} %collective-permute-done) | copy-start | bytes 786436
  41.3 29.7 %collective-permute-start.9 = (bf16[256,512]{1,0:T(8,128)(2,1)}, bf16[256,512]{1,0:T(8,128)(2,1)S(1)}, u32[]{:S(2)}, u32[]{:S(2)}) collective-permute-start(bf16[256,512]{1,0:T(8,128)(2,1)} %get-tuple-element.85), channel_id=1, source_target_pairs={{0,4},{1,5},{2,6},{3,7},{4,0},{5,1},{6,2},{7,3},{8,12},{9,13},{10,... | collective-permute-start | bytes 786440 | tf_op jit(solution)/shard_map/ppermute | solution.py:175
  54.9 48.1 %copy-start.19 = (bf16[256,512]{0,1:T(8,128)(2,1)}, bf16[256,512]{0,1:T(8,128)(2,1)S(1)}, u32[]{:S(2)}) copy-start(bf16[256,512]{0,1:T(8,128)(2,1)S(1)} %collective-permute-done.1) | copy-start | bytes 786436
  54.9 3.6 collective-permute-start.7
  55.0 48.0 %copy-start.21 = (bf16[256,512]{0,1:T(8,128)(2,1)}, bf16[256,512]{0,1:T(8,128)(2,1)S(1)}, u32[]{:S(2)}) copy-start(bf16[256,512]{0,1:T(8,128)(2,1)S(1)} %collective-permute-done.2) | copy-start | bytes 786436
  55.2 19.5 %copy-start.53 = (f32[1024]{0:T(1024)}, f32[1024]{0:T(1024)S(1)}, u32[]{:S(2)}) copy-start(f32[1024]{0:T(1024)S(1)} %broadcast_multiply_fusion.2) | copy-start | bytes 12292
  55.5 19.2 %copy-start.55 = (f32[1024]{0:T(1024)}, f32[1024]{0:T(1024)S(1)}, u32[]{:S(2)}) copy-start(f32[1024]{0:T(1024)S(1)} %fusion.30) | copy-start | bytes 12292
  55.5 15.4 %copy-start.51 = (bf16[256,512]{1,0:T(8,128)(2,1)S(1)}, bf16[256,512]{1,0:T(8,128)(2,1)}, u32[]{:S(2)}) copy-start(bf16[256,512]{1,0:T(8,128)(2,1)} %get-tuple-element.82) | copy-start | bytes 786436
  55.6 15.4 %copy-start.70 = (bf16[512,1024]{1,0:T(8,128)(2,1)S(1)}, bf16[512,1024]{1,0:T(8,128)(2,1)}, u32[]{:S(2)}) copy-start(bf16[512,1024]{1,0:T(8,128)(2,1)} %param.36) | copy-start | bytes 3145732
  57.0 19.5 %collective-permute-start.3 = (bf16[1024,1024]{1,0:T(8,128)(2,1)S(1)}, bf16[1024,1024]{1,0:T(8,128)(2,1)S(1)}, u32[]{:S(2)}, u32[]{:S(2)}) collective-permute-start(bf16[1024,1024]{1,0:T(8,128)(2,1)S(1)} %convolution_convert_fusion.4), channel_id=1, source_target_pairs={{0,1},{1,0},{2,3},{3,2},{4,5},{5,4},{6,7},{7,6},{8,9},{9,8},{10,11... | collective-permute-start | bytes 6291464 | tf_op jit(solution)/shard_map/ppermute | solution.py:194
  58.5 85.9 %collective-permute-start.15 = (bf16[256,512]{0,1:T(8,128)(2,1)}, bf16[256,512]{0,1:T(8,128)(2,1)S(1)}, u32[]{:S(2)}, u32[]{:S(2)}) collective-permute-start(bf16[256,512]{0,1:T(8,128)(2,1)} %bitcast.18), channel_id=1, source_target_pairs={{0,2},{1,3},{2,4},{3,5},{4,6},{5,7},{6,0},{7,1},{8,10},{9,11},{10,... | collective-permute-start | bytes 786440 | tf_op jit(solution)/shard_map/ppermute | solution.py:175
  67.5 77.0 %collective-permute-start.16 = (bf16[256,512]{0,1:T(8,128)(2,1)}, bf16[256,512]{0,1:T(8,128)(2,1)S(1)}, u32[]{:S(2)}, u32[]{:S(2)}) collective-permute-start(bf16[256,512]{0,1:T(8,128)(2,1)} %bitcast.19), channel_id=1, source_target_pairs={{0,4},{1,5},{2,6},{3,7},{4,0},{5,1},{6,2},{7,3},{8,12},{9,13},{10,... | collective-permute-start | bytes 786440 | tf_op jit(solution)/shard_map/ppermute | solution.py:175
  70.7 73.7 %collective-permute-start.17 = (bf16[256,512]{0,1:T(8,128)(2,1)}, bf16[256,512]{0,1:T(8,128)(2,1)}, u32[]{:S(2)}, u32[]{:S(2)}) collective-permute-start(bf16[256,512]{0,1:T(8,128)(2,1)} %bitcast.20), channel_id=1, source_target_pairs={{0,6},{1,7},{2,0},{3,1},{4,2},{5,3},{6,4},{7,5},{8,14},{9,15},{10,... | collective-permute-start | bytes 786440 | tf_op jit(solution)/shard_map/ppermute | solution.py:175
  74.7 33.8 %collective-permute-start.11 = (bf16[1024,1024]{1,0:T(8,128)(2,1)}, bf16[1024,1024]{1,0:T(8,128)(2,1)}, u32[]{:S(2)}, u32[]{:S(2)}) collective-permute-start(bf16[1024,1024]{1,0:T(8,128)(2,1)} %convolution_convert_fusion.3), channel_id=1, source_target_pairs={{0,1},{1,0},{2,3},{3,2},{4,5},{5,4},{6,7},{7,6},{8,9},{9,8},{10,11... | collective-permute-start | bytes 6291464 | tf_op jit(solution)/shard_map/ppermute | solution.py:194
  112.2 24.5 %copy-start.44 = (bf16[512,512]{1,0:T(8,128)(2,1)S(1)}, bf16[512,512]{1,0:T(8,128)(2,1)}, u32[]{:S(2)}) copy-start(bf16[512,512]{1,0:T(8,128)(2,1)} %param.37) | copy-start | bytes 1572868
  144.4 8.5 %copy-start.80 = (f32[1024,2048]{1,0:T(8,128)}, f32[1024,2048]{1,0:T(8,128)S(1)}, u32[]{:S(2)}) copy-start(f32[1024,2048]{1,0:T(8,128)S(1)} %fusion.42) | copy-start | bytes 25165828
  236.2 109.8 %collective-permute-start.22 = (bf16[1024,1024]{1,0:T(8,128)(2,1)}, bf16[1024,1024]{1,0:T(8,128)(2,1)}, u32[]{:S(2)}, u32[]{:S(2)}) collective-permute-start(bf16[1024,1024]{1,0:T(8,128)(2,1)} %slice.148), channel_id=1, source_target_pairs={{0,1},{1,0},{2,3},{3,2},{4,5},{5,4},{6,7},{7,6},{8,9},{9,8},{10,11... | collective-permute-start | bytes 6291464 | tf_op jit(solution)/shard_map/ppermute | solution.py:202
  283.5 12.8 %slice-start = ((s8[8388608]{0:T(1024)(128)(4,1)}), s8[4194304]{0:T(1024)(128)(4,1)S(1)}, s32[]{:S(2)}) async-start(s8[8388608]{0:T(1024)(128)(4,1)} %bitcast.118), calls=%async_computation.1 | async-start | bytes 8388608
  286.6 9.7 %slice-start.1 = ((s8[8388608]{0:T(1024)(128)(4,1)}), s8[4194304]{0:T(1024)(128)(4,1)S(1)}, s32[]{:S(2)}) async-start(s8[8388608]{0:T(1024)(128)(4,1)} %bitcast.118), calls=%async_computation.2 | async-start | bytes 8388608
  286.6 49.8 %collective-permute-start.18 = (bf16[1024,1024]{1,0:T(8,128)(2,1)}, bf16[1024,1024]{1,0:T(8,128)(2,1)}, u32[]{:S(2)}, u32[]{:S(2)}) collective-permute-start(bf16[1024,1024]{1,0:T(8,128)(2,1)} %slice.142), channel_id=1, source_target_pairs={{0,1},{1,0},{2,3},{3,2},{4,5},{5,4},{6,7},{7,6},{8,9},{9,8},{10,11... | collective-permute-start | bytes 6291464 | tf_op jit(solution)/shard_map/ppermute | solution.py:202
  294.6 8.3 %copy-start.82 = (bf16[1024,2048]{1,0:T(8,128)(2,1)S(1)}, bf16[1024,2048]{1,0:T(8,128)(2,1)}, u32[]{:S(2)}) copy-start(bf16[1024,2048]{1,0:T(8,128)(2,1)} %copy-done.81) | copy-start | bytes 12582916
  294.6 16.9 %collective-permute-start.12 = (bf16[256,512]{0,1:T(8,128)(2,1)}, bf16[256,512]{0,1:T(8,128)(2,1)}, u32[]{:S(2)}, u32[]{:S(2)}) collective-permute-start(bf16[256,512]{0,1:T(8,128)(2,1)} %get-tuple-element.81), channel_id=1, source_target_pairs={{0,6},{1,7},{2,0},{3,1},{4,2},{5,3},{6,4},{7,5},{8,14},{9,15},{10,... | collective-permute-start | bytes 786440 | tf_op jit(solution)/shard_map/ppermute | solution.py:186
  307.1 21.0 %collective-permute-start.13 = (bf16[256,512]{0,1:T(8,128)(2,1)}, bf16[256,512]{0,1:T(8,128)(2,1)}, u32[]{:S(2)}, u32[]{:S(2)}) collective-permute-start(bf16[256,512]{0,1:T(8,128)(2,1)} %get-tuple-element.80), channel_id=1, source_target_pairs={{0,4},{1,5},{2,6},{3,7},{4,0},{5,1},{6,2},{7,3},{8,12},{9,13},{10,... | collective-permute-start | bytes 786440 | tf_op jit(solution)/shard_map/ppermute | solution.py:186
  309.1 22.0 %collective-permute-start.14 = (bf16[256,512]{0,1:T(8,128)(2,1)}, bf16[256,512]{0,1:T(8,128)(2,1)S(1)}, u32[]{:S(2)}, u32[]{:S(2)}) collective-permute-start(bf16[256,512]{0,1:T(8,128)(2,1)} %get-tuple-element.79), channel_id=1, source_target_pairs={{0,2},{1,3},{2,4},{3,5},{4,6},{5,7},{6,0},{7,1},{8,10},{9,11},{10,... | collective-permute-start | bytes 786440 | tf_op jit(solution)/shard_map/ppermute | solution.py:186
  345.9 8.3 %copy-start.52 = (bf16[256,512]{1,0:T(8,128)(2,1)S(1)}, bf16[256,512]{1,0:T(8,128)(2,1)}, u32[]{:S(2)}) copy-start(bf16[256,512]{1,0:T(8,128)(2,1)} %get-tuple-element.82) | copy-start | bytes 786436
  345.9 8.3 %copy-start.73 = (bf16[256,512]{1,0:T(8,128)(2,1)S(1)}, bf16[256,512]{1,0:T(8,128)(2,1)}, u32[]{:S(2)}) copy-start(bf16[256,512]{1,0:T(8,128)(2,1)} %copy-done.72) | copy-start | bytes 786436
  351.9 87.7 %collective-permute-start.23 = (bf16[256,512]{1,0:T(8,128)(2,1)}, bf16[256,512]{1,0:T(8,128)(2,1)}, u32[]{:S(2)}, u32[]{:S(2)}) collective-permute-start(bf16[256,512]{1,0:T(8,128)(2,1)} %get-tuple-element.71), channel_id=1, source_target_pairs={{0,6},{1,7},{2,0},{3,1},{4,2},{5,3},{6,4},{7,5},{8,14},{9,15},{10,... | collective-permute-start | bytes 786440 | tf_op jit(solution)/shard_map/ppermute | solution.py:186
  351.9 93.4 %collective-permute-start.24 = (bf16[256,512]{1,0:T(8,128)(2,1)}, bf16[256,512]{1,0:T(8,128)(2,1)}, u32[]{:S(2)}, u32[]{:S(2)}) collective-permute-start(bf16[256,512]{1,0:T(8,128)(2,1)} %get-tuple-element.70), channel_id=1, source_target_pairs={{0,4},{1,5},{2,6},{3,7},{4,0},{5,1},{6,2},{7,3},{8,12},{9,13},{10,... | collective-permute-start | bytes 786440 | tf_op jit(solution)/shard_map/ppermute | solution.py:186
  352.0 95.1 %collective-permute-start.25 = (bf16[256,512]{1,0:T(8,128)(2,1)}, bf16[256,512]{1,0:T(8,128)(2,1)}, u32[]{:S(2)}, u32[]{:S(2)}) collective-permute-start(bf16[256,512]{1,0:T(8,128)(2,1)} %get-tuple-element.69), channel_id=1, source_target_pairs={{0,2},{1,3},{2,4},{3,5},{4,6},{5,7},{6,0},{7,1},{8,10},{9,11},{10,... | collective-permute-start | bytes 786440 | tf_op jit(solution)/shard_map/ppermute | solution.py:186
  370.9 57.6 %collective-permute-start.19 = (bf16[256,512]{0,1:T(8,128)(2,1)S(1)}, bf16[256,512]{0,1:T(8,128)(2,1)S(1)}, u32[]{:S(2)}, u32[]{:S(2)}) collective-permute-start(bf16[256,512]{0,1:T(8,128)(2,1)S(1)} %get-tuple-element.74), channel_id=1, source_target_pairs={{0,6},{1,7},{2,0},{3,1},{4,2},{5,3},{6,4},{7,5},{8,14},{9,15},{10,... | collective-permute-start | bytes 786440 | tf_op jit(solution)/shard_map/ppermute | solution.py:186
  373.3 56.0 %collective-permute-start.20 = (bf16[256,512]{0,1:T(8,128)(2,1)}, bf16[256,512]{0,1:T(8,128)(2,1)S(1)}, u32[]{:S(2)}, u32[]{:S(2)}) collective-permute-start(bf16[256,512]{0,1:T(8,128)(2,1)} %get-tuple-element.73), channel_id=1, source_target_pairs={{0,4},{1,5},{2,6},{3,7},{4,0},{5,1},{6,2},{7,3},{8,12},{9,13},{10,... | collective-permute-start | bytes 786440 | tf_op jit(solution)/shard_map/ppermute | solution.py:186
  428.5 10.1 %collective-permute-start.21 = (bf16[256,512]{0,1:T(8,128)(2,1)}, bf16[256,512]{0,1:T(8,128)(2,1)S(1)}, u32[]{:S(2)}, u32[]{:S(2)}) collective-permute-start(bf16[256,512]{0,1:T(8,128)(2,1)} %get-tuple-element.72), channel_id=1, source_target_pairs={{0,2},{1,3},{2,4},{3,5},{4,6},{5,7},{6,0},{7,1},{8,10},{9,11},{10,... | collective-permute-start | bytes 786440 | tf_op jit(solution)/shard_map/ppermute | solution.py:186
  (66 other events, 249.9 us)
Sparse Core Ops, SparseCore 0:
  361.7 209.4 all-reduce.3

commit v2 on v1

v2 whole, which is shorter than its diff:
```python
import functools
import math

import jax
import jax.numpy as jnp
from jax import lax
from jax.experimental import pallas as pl
from jax.experimental.pallas import tpu as pltpu
from jax.sharding import PartitionSpec as P

HEADS = 8
NT = (((1,), (1,)), ((), ()))
NN = (((1,), (0,)), ((), ()))
TN = (((0,), (0,)), ((), ()))
f32 = jnp.float32
bf16 = jnp.bfloat16
VMEM = 60 * 1024 * 1024
QUERY_SCALE = 0.125 * math.log2(math.e)
HIDDEN_MASK = -1e30


def dot(left, right, dims=NN):
    return lax.dot_general(left, right, dims, preferred_element_type=f32)


def normalize(values):
    centered = values - jnp.mean(values, axis=1, keepdims=True)
    inverse = lax.rsqrt(jnp.mean(centered * centered, axis=1, keepdims=True) + 1e-05)
    return centered * inverse, inverse


def normalize_back(grad, normal, inverse, gain):
    grad = grad * gain
    shift = jnp.mean(grad, axis=1, keepdims=True)
    along = jnp.mean(grad * normal, axis=1, keepdims=True)
    return inverse * (grad - shift - normal * along)


def column_sums(values):
    return jnp.sum(values, axis=0, keepdims=True)


def whole(array, *index):
    shape = array.shape
    index = index or (0,) * len(shape)
    return pl.BlockSpec(shape, lambda *grid: index)


def shaped(shape, dtype=bf16):
    return jax.ShapeDtypeStruct(shape, dtype)


def run(kernel, name, operands, outs, flops, limit=60):
    specs, arrays = [], []
    for operand in operands:
        if isinstance(operand, tuple):
            array, width, column = operand
            specs.append(whole(shaped((array.shape[0], width)), 0, column))
        else:
            array = operand
            specs.append(whole(array))
        arrays.append(array)
    size = sum(item.size * item.dtype.itemsize for item in arrays + list(outs))
    return pl.pallas_call(
        kernel,
        grid=(1,),
        in_specs=specs,
        out_specs=[whole(out) for out in outs],
        out_shape=list(outs),
        compiler_params=pltpu.CompilerParams(vmem_limit_bytes=limit * 1024 * 1024),
        cost_estimate=pl.CostEstimate(flops=flops, bytes_accessed=size, transcendentals=0),
        name=name,
    )(*arrays)


def forward_kernel(parts, *refs):
    q_ref, qmask_ref = refs[:2]
    k_refs, v_refs, kmask_refs = (refs[2 + i * parts : 2 + (i + 1) * parts] for i in range(3))
    o_ref, lse_ref = refs[2 + 3 * parts :]
    low = lax.broadcasted_iota(jnp.int32, (1, 128), 1) < 64
    k = jnp.concatenate([ref[...] for ref in k_refs], 0)
    v = jnp.concatenate([ref[...] for ref in v_refs], 0)
    kmask = jnp.concatenate([ref[...] for ref in kmask_refs], 0)
    q, qmask = q_ref[...], qmask_ref[...]
    outputs = []
    for head in range(2):
        mine = low if head == 0 else ~low
        scores = dot(jnp.where(mine, k, kmask), jnp.where(mine, q, qmask), NT)
        largest = jnp.max(scores, axis=0, keepdims=True)
        weights = jnp.exp2(scores - largest).astype(bf16)
        both = dot(jnp.where(mine, v, jnp.ones_like(v)), weights, TN)
        total = both[64 - head * 64 : 65 - head * 64]
        lse_ref[0, head : head + 1, :] = largest + jnp.log2(total)
        outputs.append(both[head * 64 : head * 64 + 64] / total)
    o_ref[...] = jnp.concatenate(outputs, 0).T.astype(bf16)


def columns(rows, column, count):
    if callable(column):
        return [pl.BlockSpec((rows, 128), lambda h: (0, column(h)))] * count
    return [pl.BlockSpec((rows, 128), lambda h: (0, column))] * count


def attend(queries, qmask, keyvals, masks, mask_column):
    tokens, features = queries.shape
    parts = len(keyvals)
    length = parts * tokens
    pairs = features // 128
    of_queries = pl.BlockSpec((tokens, 128), lambda h: (0, h))
    return pl.pallas_call(
        functools.partial(forward_kernel, parts),
        grid=(pairs,),
        in_specs=[of_queries]
        + columns(tokens, 0, 1)
        + columns(tokens, lambda h: h, parts)
        + columns(tokens, lambda h: h + pairs, parts)
        + columns(tokens, mask_column, parts),
        out_specs=[of_queries, pl.BlockSpec((1, 2, tokens), lambda h: (h, 0, 0))],
        out_shape=[shaped((tokens, features)), shaped((pairs, 2, tokens), f32)],
        compiler_params=pltpu.CompilerParams(vmem_limit_bytes=VMEM),
        cost_estimate=pl.CostEstimate(
            flops=HEADS * 4 * tokens * length * 128,
            bytes_accessed=2 * features * (2 * tokens + 2 * length),
            transcendentals=HEADS * tokens * length,
        ),
        name="attend",
    )(queries, qmask, *keyvals, *keyvals, *masks)


def backward_kernel(parts, *refs):
    q_ref, qmask_ref, do_ref, o_ref, lse_ref = refs[:5]
    k_refs, v_refs, kmask_refs = (refs[5 + i * parts : 5 + (i + 1) * parts] for i in range(3))
    dq_ref, dkv_refs = refs[5 + 3 * parts], refs[6 + 3 * parts :]
    low = lax.broadcasted_iota(jnp.int32, (1, 128), 1) < 64
    q, qmask, grad = q_ref[...], qmask_ref[...], do_ref[...]
    tokens = q.shape[0]
    product = grad.astype(f32) * o_ref[...].astype(f32)
    upper = product.astype(bf16)
    lower = (product - upper.astype(f32)).astype(bf16)
    rows = lax.broadcasted_iota(jnp.int32, (8, 128), 0)
    lanes = lax.broadcasted_iota(jnp.int32, (8, 128), 1)
    pick = jnp.where(rows == lanes // 64, 1.0, 0.0).astype(bf16)
    delta = dot(pick, upper, NT) + dot(pick, lower, NT)
    lse = lse_ref[0]
    zero = jnp.zeros_like(grad)
    q_heads = [jnp.where(low, q, qmask), jnp.where(low, qmask, q)]
    grad_heads = [jnp.where(low, grad, zero), jnp.where(low, zero, grad)]
    dq = [jnp.zeros((64, tokens), f32)] * 2
    for part in range(parts):
        k, v = k_refs[part][...], v_refs[part][...]
        kmask = kmask_refs[part][...]
        dk, dv = [], []
        for head in range(2):
            k_head = jnp.where(low, k, kmask) if head == 0 else jnp.where(low, kmask, k)
            weights = jnp.exp2(dot(k_head, q_heads[head], NT) - lse[head : head + 1, :])
            grad_weights = dot(v, grad_heads[head], NT)
            grad_scores = (weights * (grad_weights - delta[head : head + 1, :])).astype(bf16)
            dv.append(dot(weights.astype(bf16), grad))
            dk.append(dot(grad_scores, q))
            dq[head] = dq[head] + dot(k, grad_scores, TN)[head * 64 : head * 64 + 64]
        dkv_refs[part][:, :128] = (jnp.where(low, dk[0], dk[1]) * math.log(2.0)).astype(bf16)
        dkv_refs[part][:, 128:] = jnp.where(low, dv[0], dv[1]).astype(bf16)
    dq_ref[...] = (jnp.concatenate(dq, 0).T * 0.125).astype(bf16)


def attend_back(queries, qmask, grad, outputs, lse, keyvals, masks, mask_column, first, count):
    tokens, features = queries.shape
    parts = len(keyvals)
    length = parts * tokens
    pairs = features // 128
    of_queries = pl.BlockSpec((tokens, 128), lambda h: (0, h + first))
    return pl.pallas_call(
        functools.partial(backward_kernel, parts),
        grid=(count,),
        in_specs=[
            of_queries,
            pl.BlockSpec((tokens, 128), lambda h: (0, 0)),
            of_queries,
            of_queries,
            pl.BlockSpec((1, 2, tokens), lambda h: (h + first, 0, 0)),
        ]
        + columns(tokens, lambda h: h + first, parts)
        + columns(tokens, lambda h: h + first + pairs, parts)
        + columns(tokens, mask_column, parts),
        out_specs=[pl.BlockSpec((tokens, 128), lambda h: (0, h))]
        + [pl.BlockSpec((tokens, 256), lambda h: (0, h))] * parts,
        out_shape=[shaped((tokens, count * 128))] + [shaped((tokens, count * 256))] * parts,
        compiler_params=pltpu.CompilerParams(vmem_limit_bytes=VMEM),
        cost_estimate=pl.CostEstimate(
            flops=count * 20 * tokens * length * 128,
            bytes_accessed=2 * count * 128 * (4 * tokens + 4 * length),
            transcendentals=2 * count * tokens * length,
        ),
        name="attend_back",
    )(queries, qmask, grad, outputs, lse, *keyvals, *keyvals, *masks)


def mask_rows(codes, of_queries):
    places = lax.broadcasted_iota(jnp.int32, (128, codes.shape[1]), 0) % 64
    codes = jnp.broadcast_to(codes.astype(jnp.int32), places.shape)
    if of_queries:
        mask = jnp.where(codes % 4 == places, 1.0, 0.0)
    else:
        mask = jnp.where((codes != places) & (places < 3), HIDDEN_MASK, 0.0)
    return mask.T.astype(bf16)


def project_kernel(parts, length, *refs):
    x_refs = refs[:parts]
    gain_ref, bias_ref, w_ref, x_ref, normed_ref, query_ref, keyvals_ref, qmask_ref = refs[parts:]
    features = x_ref.shape[1]
    for part in range(parts):
        rows = slice(part * length, (part + 1) * length)
        low = x_refs[part][:length, :]
        x_ref[rows, :] = low
        normal, inverse = normalize(low.astype(f32))
        normed = (normal * gain_ref[...] + bias_ref[...]).astype(bf16)
        normed_ref[rows, :] = normed
        projected = dot(normed, w_ref[...])
        query_ref[rows, :] = (projected[:, :features] * QUERY_SCALE).astype(bf16)
        keyvals_ref[rows, : 2 * features] = projected[:, features:].astype(bf16)
        codes = x_refs[part][length : length + 16, :].astype(f32)[0:1, :]
        qmask_ref[rows, :] = mask_rows(codes[:, :length], True)
        keyvals_ref[rows, 2 * features : 2 * features + 128] = mask_rows(codes[:, :length], False)
        keyvals_ref[rows, 2 * features + 128 :] = mask_rows(codes[:, length : 2 * length], False)


def row_specs(array, count):
    shape = (1,) + array.shape[1:]
    return [
        pl.BlockSpec(shape, lambda i, row, step=step: ((row[0] + step) % count, 0, 0)) for step in range(count)
    ]


def pack_target(row, target, codes):
    count, length, features = target.shape

    def kernel(row_ref, *refs):
        seg_ref, keep_ref, memory_seg_ref, memory_keep_ref = refs[count : count + 4]
        for step in range(count):
            out_ref = refs[count + 4 + step]
            out_ref[:length, :] = refs[step][0]
            which = pl.ds((row_ref[0] + step) % count, 1)
            pieces = [
                jnp.where(keep[which, :] == 1, seg[which, :], seg[which, :] + 4).astype(f32)
                for seg, keep in ((seg_ref, keep_ref), (memory_seg_ref, memory_keep_ref))
            ]
            if features > 2 * length:
                pieces.append(jnp.zeros((1, features - 2 * length), f32))
            pieces = jnp.concatenate(pieces, 1)
            out_ref[length:, :] = jnp.broadcast_to(pieces, (16, features)).astype(bf16)

    out = shaped((length + 16, features))
    return pl.pallas_call(
        kernel,
        grid_spec=pltpu.PrefetchScalarGridSpec(
            num_scalar_prefetch=1,
            grid=(1,),
            in_specs=row_specs(target, count) + [whole(item) for item in codes],
            out_specs=[whole(out)] * count,
        ),
        out_shape=[out] * count,
        compiler_params=pltpu.CompilerParams(vmem_limit_bytes=VMEM),
        name="pack_target",
    )(row.reshape(1), *[target] * count, *codes)


def pack_rows(row, arrays):
    count, length, features = arrays[0].shape
    total = count * len(arrays)

    def kernel(row_ref, *refs):
        for i in range(total):
            refs[total + i][...] = refs[i][0]

    out = shaped((length, features), arrays[0].dtype)
    outs = pl.pallas_call(
        kernel,
        grid_spec=pltpu.PrefetchScalarGridSpec(
            num_scalar_prefetch=1,
            grid=(1,),
            in_specs=[spec for array in arrays for spec in row_specs(array, count)],
            out_specs=[whole(out)] * total,
        ),
        out_shape=[out] * total,
        compiler_params=pltpu.CompilerParams(vmem_limit_bytes=VMEM),
        name="pack_rows",
    )(row.reshape(1), *[array for array in arrays for _ in range(count)])
    return [tuple(outs[i : i + count]) for i in range(0, total, count)]


def place_rows(row, parts):
    count = len(parts)
    length, features = parts[0].shape

    def kernel(row_ref, *refs):
        for step in range(count):

            @pl.when(pl.program_id(0) == step)
            def _():
                refs[count][0] = refs[step][...].astype(f32)

    return pl.pallas_call(
        kernel,
        grid_spec=pltpu.PrefetchScalarGridSpec(
            num_scalar_prefetch=1,
            grid=(count,),
            in_specs=[pl.BlockSpec((length, features), lambda i, row: (0, 0))] * count,
            out_specs=pl.BlockSpec((1, length, features), lambda i, row: ((row[0] + i) % count, 0, 0)),
        ),
        out_shape=shaped((count, length, features), f32),
        name="place_rows",
    )(row.reshape(1), *parts)


def unpack_feed(place, parts, hidden, block):
    share = len(parts)
    features = parts[0].shape[1]
    steps = hidden // block
    each = steps // share

    def kernel(place_ref, *refs):
        up_ref, down_ref = refs[share:]
        owner = pl.program_id(0) // each
        for step in range(share):

            @pl.when((place_ref[0] + share - owner) % share == step)
            def _():
                up_ref[...] = refs[step][:features, :].astype(f32)
                down_ref[...] = refs[step][features:, :].astype(f32)

    return pl.pallas_call(
        kernel,
        grid_spec=pltpu.PrefetchScalarGridSpec(
            num_scalar_prefetch=1,
            grid=(steps,),
            in_specs=[pl.BlockSpec((2 * features, features), lambda j, place: (j % each, 0))] * share,
            out_specs=[
                pl.BlockSpec((features, block), lambda j, place: (0, j)),
                pl.BlockSpec((block, features), lambda j, place: (j, 0)),
            ],
        ),
        out_shape=[shaped((features, hidden), f32), shaped((hidden, features), f32)],
        compiler_params=pltpu.CompilerParams(vmem_limit_bytes=VMEM),
        name="unpack_feed",
    )(place.reshape(1), *parts)


def unpack_columns(place, parts, widths):
    share = len(parts)
    rows = parts[0].shape[0]

    def kernel(place_ref, *refs):
        for step in range(share):

            @pl.when((place_ref[0] + share - pl.program_id(0)) % share == step)
            def _():
                start = 0
                for width, out_ref in zip(widths, refs[share:]):
                    out_ref[...] = refs[step][:, start : start + width].astype(f32)
                    start += width

    return pl.pallas_call(
        kernel,
        grid_spec=pltpu.PrefetchScalarGridSpec(
            num_scalar_prefetch=1,
            grid=(share,),
            in_specs=[pl.BlockSpec(part.shape, lambda j, place: (0, 0)) for part in parts],
            out_specs=[pl.BlockSpec((rows, width), lambda j, place: (j, 0)) for width in widths],
        ),
        out_shape=[shaped((share * rows, width), f32) for width in widths],
        compiler_params=pltpu.CompilerParams(vmem_limit_bytes=VMEM),
        name="unpack_columns",
    )(place.reshape(1), *parts)


def memory_kernel(parts, *refs):
    part_refs = refs[:parts]
    w_ref, memory_ref, keyvals_ref = refs[parts:]
    length = part_refs[0].shape[0]
    for part in range(parts):
        rows = slice(part * length, (part + 1) * length)
        memory = part_refs[part][...]
        memory_ref[rows, :] = memory
        keyvals_ref[rows, :] = dot(memory, w_ref[...]).astype(bf16)


def after_self_kernel(x_ref, attended_ref, w_out_ref, gain_ref, bias_ref, w_q_ref, after_ref, normed_ref, query_ref):
    after = x_ref[...].astype(f32) + dot(attended_ref[...], w_out_ref[...])
    after_ref[...] = after
    normal, inverse = normalize(after)
    normed = (normal * gain_ref[...] + bias_ref[...]).astype(bf16)
    normed_ref[...] = normed
    query_ref[...] = (dot(normed, w_q_ref[...]) * QUERY_SCALE).astype(bf16)


def feed_kernel(parts, share, each, place_ref, *refs):
    after_ref, attended_ref, w_out_ref, gain_ref, bias_ref, w_up_ref, b_up_ref, w_down_ref, b_down_ref = refs[:9]
    cotangent_refs, refs = refs[9 : 9 + parts], refs[9 + parts :]
    out_refs, grad_w_refs, refs = refs[:parts], refs[parts : parts + share], refs[parts + share :]
    grad_ref, grad_heads_ref, grad_out_ref, grad_b_up_ref, sums_ref = refs[:5]
    normed_ref, x_ref, total_ref, back_ref, cotangent_ref = refs[5:]
    features = w_up_ref.shape[0]
    length = out_refs[0].shape[0]
    step = pl.program_id(0)

    @pl.when(step == 0)
    def _():
        for part, part_ref in enumerate(cotangent_refs):
            cotangent_ref[part * length : (part + 1) * length, :] = part_ref[...]
        x = after_ref[...] + dot(attended_ref[...], w_out_ref[...])
        x_ref[...] = x
        total_ref[...] = x + b_down_ref[...]
        normal, inverse = normalize(x)
        normed_ref[...] = (normal * gain_ref[...] + bias_ref[...]).astype(bf16)
        back_ref[...] = jnp.zeros_like(back_ref)

    cotangent = cotangent_ref[...]
    normed, w_up, w_down = normed_ref[...], w_up_ref[...], w_down_ref[...]
    u = dot(normed, w_up) + b_up_ref[...]
    slope = math.sqrt(2.0 / math.pi)
    squared = u * u
    bent = jnp.tanh(u * (slope + slope * 0.044715 * squared))
    half = 0.5 + 0.5 * bent
    activated = (u * half).astype(bf16)
    gelu_slope = half + (0.5 * u) * (1.0 - bent * bent) * (slope + 3.0 * slope * 0.044715 * squared)
    total_ref[...] += dot(activated, w_down)
    grad_hidden = (dot(cotangent, w_down, NT) * gelu_slope).astype(bf16)
    grad_up = dot(normed, grad_hidden, TN).astype(bf16)
    grad_down = dot(activated, cotangent, TN).astype(bf16)
    for part, grad_w_ref in enumerate(grad_w_refs):

        @pl.when(step // each == share - 1 - part)
        def _():
            grad_w_ref[:features, :] = grad_up
            grad_w_ref[features:, :] = grad_down

    grad_b_up_ref[...] = column_sums(grad_hidden.astype(f32))
    back_ref[...] += dot(grad_hidden, w_up, NT)

    @pl.when(step == pl.num_programs(0) - 1)
    def _():
        for part, out_ref in enumerate(out_refs):
            out_ref[...] = total_ref[part * length : (part + 1) * length, :].astype(bf16)
        normal, inverse = normalize(x_ref[...])
        grad_normed = back_ref[...]
        grad_out = cotangent.astype(f32)
        sums_ref[0:1, :] = column_sums(grad_normed * normal)
        sums_ref[1:2, :] = column_sums(grad_normed)
        sums_ref[2:3, :] = column_sums(grad_out)
        grad = grad_out + normalize_back(grad_normed, normal, inverse, gain_ref[...])
        grad_ref[...] = grad
        low = grad.astype(bf16)
        grad_heads_ref[...] = dot(low, w_out_ref[...], NT).astype(bf16)
        grad_out_ref[...] = dot(attended_ref[...], low, TN).astype(bf16)


def feed_forward(place, share, after_self, attended, cotangents, w_out, gain, bias, w_up, b_up, w_down, b_down):
    tokens, features = after_self.shape
    hidden = w_up.shape[1]
    block = features
    parts = len(cotangents)
    length = tokens // parts
    steps = hidden // block
    each = steps // share
    row, one, square = shaped((tokens, features)), shaped((1, features)), shaped((features, features))
    part_row = shaped((length, features))

    def now(j, place):
        return ((place[0] + share - 1 - j // each) % share) * each + j % each

    def grad_spec(part):
        begin = (share - 1 - part) * each
        return pl.BlockSpec(
            (features + block, features), lambda j, place: (jnp.clip(j - begin, 0, each - 1), 0)
        )

    return pl.pallas_call(
        functools.partial(feed_kernel, parts, share, each),
        grid_spec=pltpu.PrefetchScalarGridSpec(
            num_scalar_prefetch=1,
            grid=(steps,),
            in_specs=[
                whole(row),
                whole(row),
                whole(square),
                whole(one),
                whole(one),
                pl.BlockSpec((features, block), lambda j, place: (0, now(j, place))),
                pl.BlockSpec((1, block), lambda j, place: (0, now(j, place))),
                pl.BlockSpec((block, features), lambda j, place: (now(j, place), 0)),
                whole(one),
            ]
            + [whole(part_row)] * parts,
            out_specs=[whole(part_row)] * parts
            + [grad_spec(part) for part in range(share)]
            + [
                whole(row),
                whole(row),
                whole(square),
                pl.BlockSpec((1, block), lambda j, place: (0, now(j, place))),
                whole(shaped((8, features))),
            ],
            scratch_shapes=[
                pltpu.VMEM((tokens, features), bf16),
                pltpu.VMEM((tokens, features), f32),
                pltpu.VMEM((tokens, features), f32),
                pltpu.VMEM((tokens, features), f32),
                pltpu.VMEM((tokens, features), bf16),
            ],
        ),
        out_shape=[part_row] * parts
        + [shaped((each * (features + block), features))] * share
        + [
            shaped((tokens, features), f32),
            row,
            square,
            shaped((1, hidden), f32),
            shaped((8, features), f32),
        ],
        compiler_params=pltpu.CompilerParams(vmem_limit_bytes=VMEM),
        cost_estimate=pl.CostEstimate(
            flops=2 * tokens * features * (6 * hidden + 3 * features),
            bytes_accessed=12 * features * hidden + 20 * tokens * features,
            transcendentals=tokens * hidden,
        ),
        name="feed_forward",
    )(place.reshape(1), after_self, attended, w_out, gain, bias, w_up, b_up, w_down, b_down, *cotangents)


def after_self_back_kernel(calls, *refs):
    dq_refs = refs[:calls]
    after_ref, normed_ref, attended_ref, grad_after_ref, gain_ref, w_q_ref, w_out_ref = refs[calls : calls + 7]
    grad_ref, grad_heads_ref, grad_w_ref, sums_ref = refs[calls + 7 :]
    features = after_ref.shape[1]
    grad_query = jnp.concatenate([ref[...] for ref in dq_refs], 1)
    grad_normed = dot(grad_query, w_q_ref[...], NT)
    normal, inverse = normalize(after_ref[...])
    sums_ref[0:1, :] = column_sums(grad_normed * normal)
    sums_ref[1:2, :] = column_sums(grad_normed)
    grad = grad_after_ref[...] + normalize_back(grad_normed, normal, inverse, gain_ref[...])
    grad_ref[...] = grad
    low = grad.astype(bf16)
    grad_heads_ref[...] = dot(low, w_out_ref[...], NT).astype(bf16)
    grad_w_ref[:, :features] = dot(normed_ref[...], grad_query, TN).astype(bf16)
    grad_w_ref[:, features:] = dot(attended_ref[...], low, TN).astype(bf16)


def summed_keyvals(refs):
    keys, values = [], []
    for call in refs:
        total = sum([ref[...].astype(f32) for ref in call[1:]], call[0][...].astype(f32)).astype(bf16)
        for pair in range(total.shape[1] // 256):
            keys.append(total[:, pair * 256 : pair * 256 + 128])
            values.append(total[:, pair * 256 + 128 : pair * 256 + 256])
    return keys + values


def memory_back_kernel(calls, parts, *refs):
    grad_refs = [refs[call * parts : (call + 1) * parts] for call in range(calls)]
    memory_ref, w_ref, out_ref, pair_ref, grad_w_ref = refs[calls * parts : calls * parts + 5]
    row_refs = refs[calls * parts + 5 :]
    features = out_ref.shape[1]
    grad = jnp.concatenate(summed_keyvals(grad_refs), 1)
    result = dot(grad, w_ref[...], NT).astype(bf16)
    length = row_refs[0].shape[0]
    for part, row_ref in enumerate(row_refs):
        row_ref[...] = result[part * length : (part + 1) * length, :]
    grad_w_ref[:, :features] = out_ref[...]
    grad_w_ref[:, features : 3 * features] = pair_ref[...]
    grad_w_ref[:, 3 * features :] = dot(memory_ref[...], grad, TN).astype(bf16)


def project_back_kernel(calls, parts, *refs):
    dq_refs = refs[:calls]
    refs = refs[calls:]
    grad_refs = [refs[call * parts : (call + 1) * parts] for call in range(calls)]
    refs = refs[calls * parts :]
    x_ref, normed_ref, gain_ref, w_ref, grad_after_ref, second_ref, third_ref, b_up_ref, grad_w_ref, sums_ref = refs[:10]
    row_refs = refs[10:]
    grad = jnp.concatenate([ref[...] for ref in dq_refs] + summed_keyvals(grad_refs), 1)
    grad_w_ref[...] = dot(normed_ref[...], grad, TN).astype(bf16)
    grad_normed = dot(grad, w_ref[...], NT)
    normal, inverse = normalize(x_ref[...].astype(f32))
    result = grad_after_ref[...] + normalize_back(grad_normed, normal, inverse, gain_ref[...])
    length = row_refs[0].shape[0]
    for part, row_ref in enumerate(row_refs):
        row_ref[...] = result[part * length : (part + 1) * length, :].astype(bf16)
    sums_ref[...] = jnp.zeros_like(sums_ref)
    width, features = sums_ref.shape[1], x_ref.shape[1]
    pieces = [column_sums(grad_normed * normal), column_sums(grad_normed), second_ref[0:1, :], second_ref[1:2, :]]
    pieces += [third_ref[0:1, :], third_ref[1:2, :], third_ref[2:3, :]]
    pieces += [b_up_ref[:, i : i + features] for i in range(0, b_up_ref.shape[1], features)]
    for i, piece in enumerate(pieces):
        row, column = divmod(i * features, width)
        sums_ref[row : row + 1, column : column + features] = piece.astype(bf16)


class Layout:
    def __init__(self, dp, rows, blocks):
        self.rows = rows
        self.share = share = blocks // rows
        self.blocks = blocks
        self.dp = dp
        place = lax.axis_index("blk")
        self.row = place // share
        self.place = lax.rem(place, share)

    def shift_rows(self, step):
        rows, share = self.rows, self.share
        return [
            (a * share + b, ((a + step) % rows) * share + b) for a in range(rows) for b in range(share)
        ]

    def shift_share(self, step):
        rows, share = self.rows, self.share
        return [
            (a * share + b, a * share + (b + step) % share) for a in range(rows) for b in range(share)
        ]

    def bring_rows(self, parts):
        return (parts[0],) + tuple(
            lax.ppermute(parts[step], "blk", self.shift_rows(step)) for step in range(1, self.rows)
        )

    def return_rows(self, parts):
        return (parts[0],) + tuple(
            lax.ppermute(parts[step], "blk", self.shift_rows(self.rows - step)) for step in range(1, self.rows)
        )

    def gather_share(self, values):
        return (values,) + tuple(
            lax.ppermute(values, "blk", self.shift_share(step)) for step in range(1, self.share)
        )

    def return_share(self, parts):
        return (parts[0],) + tuple(
            lax.ppermute(parts[step], "blk", self.shift_share(self.share - step))
            for step in range(1, self.share)
        )


class Sum:
    def __init__(self, layout, values, extra=None):
        share, rows, dp = layout.share, layout.rows, layout.dp
        place = lax.axis_index("blk")
        levels = [
            ("blk", share, lax.rem(place, share), layout.shift_share),
            ("dp", dp, lax.axis_index("dp"), lambda step: [(d, (d + step) % dp) for d in range(dp)]),
            ("blk", rows, place // share, layout.shift_rows),
        ]
        self.values = values
        self.extra = extra
        self.left = [(self.scatter,) + level for level in levels]
        self.left += [(self.gather,) + level for level in reversed(levels)]

    def scatter(self, axis, count, index, shift):
        if isinstance(self.values, tuple):
            parts = self.values
            total = parts[0].astype(f32)
            for step in range(1, count):
                total = total + lax.ppermute(parts[step], axis, shift(step)).astype(f32)
            self.values = total.astype(bf16)
            return
        part_rows = self.values.shape[0] // count

        def part(which):
            return lax.dynamic_slice_in_dim(self.values, which * part_rows, part_rows, 0)

        total = part(index).astype(f32)
        extra = None if self.extra is None else self.extra.astype(f32)
        arrived = []
        for step in range(1, count):
            send = part(lax.rem(index + step, count))
            if extra is not None:
                send = jnp.concatenate([send, self.extra], 0)
            arrived.append(lax.ppermute(send, axis, shift(step)))
        for item in arrived:
            total = total + item[:part_rows].astype(f32)
            if extra is not None:
                extra = extra + item[part_rows:].astype(f32)
        self.values = total.astype(bf16)
        if extra is not None:
            self.extra = extra.astype(bf16)

    def gather(self, axis, count, index, shift):
        mine = self.values
        part_rows = mine.shape[0]
        arrived = [lax.ppermute(mine, axis, shift(step)) for step in range(1, count)]
        if not self.left:
            self.values = (mine, *arrived)
            return
        result = jnp.zeros((count * part_rows, mine.shape[1]), mine.dtype)
        result = lax.dynamic_update_slice_in_dim(result, mine, index * part_rows, 0)
        for step, item in enumerate(arrived, 1):
            source = lax.rem(index + count - step, count)
            result = lax.dynamic_update_slice_in_dim(result, item, source * part_rows, 0)
        self.values = result

    def step(self):
        action = self.left.pop(0)
        action[0](*action[1:])


def join(*values):
    return lax.optimization_barrier(values)


def body(
    dp,
    blocks,
    target,
    memory,
    target_seg,
    target_keep,
    memory_seg,
    memory_keep,
    cotangent,
    norm1_gain,
    norm1_bias,
    w_qkv,
    w_out,
    norm2_gain,
    norm2_bias,
    w_cross_q,
    w_cross_kv,
    w_cross_out,
    norm3_gain,
    norm3_bias,
    w_up,
    b_up,
    w_down,
    b_down,
):
    rows, length, features = target.shape
    tokens = rows * length
    layout = Layout(dp, rows, blocks)
    target_parts = pack_target(layout.row, target, (target_seg, target_keep, memory_seg, memory_keep))
    target_parts = layout.bring_rows(target_parts)
    memory_parts, cotangent_parts = pack_rows(layout.row, (memory, cotangent))
    norm1_gain, norm1_bias, norm2_gain, norm2_bias, norm3_gain, norm3_bias, b_up, b_down = (
        item.reshape(1, -1)
        for item in (norm1_gain, norm1_bias, norm2_gain, norm2_bias, norm3_gain, norm3_bias, b_up, b_down)
    )
    hidden = w_up.shape[1]
    row, wide_row, full_row = (shaped((tokens, features)), shaped((tokens, 2 * features)), shaped((tokens, features), f32))
    row_parts = (shaped((length, features)),) * rows
    sums = shaped((8, features), f32)
    unit = 2 * tokens * features * features
    pairs = features // 128

    x, normed1, queries, keyvals, qmask = run(
        functools.partial(project_kernel, rows, length),
        "project",
        target_parts + (norm1_gain, norm1_bias, w_qkv),
        (row, row, row, shaped((tokens, 2 * features + 256)), shaped((tokens, 128))),
        3 * unit,
    )
    keyvals, memory_parts = join(keyvals, memory_parts)
    keyvals = layout.gather_share(keyvals)
    memory_parts = layout.bring_rows(memory_parts)
    self_masks = (keyvals, 2 * pairs)
    cross_masks = (keyvals, 2 * pairs + 1)
    self_low, self_lse = attend(queries, qmask, keyvals, *self_masks)
    self_low, memory_parts, cotangent_parts = join(self_low, memory_parts, cotangent_parts)
    memory_row, memory_keyvals = run(
        functools.partial(memory_kernel, rows), "memory", memory_parts + (w_cross_kv,), (row, wide_row), 2 * unit
    )
    memory_keyvals = layout.gather_share(memory_keyvals)
    after_self, normed2, cross_query = run(
        after_self_kernel,
        "after_self",
        (x, self_low, w_out, norm2_gain, norm2_bias, w_cross_q),
        (full_row, row, row),
        2 * unit,
    )
    cross_query, cotangent_parts, memory_keyvals = join(cross_query, cotangent_parts, memory_keyvals)
    cotangent_parts = layout.bring_rows(cotangent_parts)
    cross_low, cross_lse = attend(cross_query, qmask, memory_keyvals, *cross_masks)
    cross_low, cotangent_parts = join(cross_low, cotangent_parts)
    fed = feed_forward(
        layout.place,
        layout.share,
        after_self,
        cross_low,
        cotangent_parts,
        w_cross_out,
        norm3_gain,
        norm3_bias,
        w_up,
        b_up,
        w_down,
        b_down,
    )
    block_parts, grad_feed = tuple(fed[:rows]), tuple(fed[rows : rows + layout.share])
    grad_after_cross, grad_cross_heads, grad_w_cross_out, grad_b_up, sums3 = fed[rows + layout.share :]

    calls = 2
    count = pairs // calls
    first = Sum(layout, grad_feed)
    operands = (cross_query, qmask, grad_cross_heads, cross_low, cross_lse, memory_keyvals) + cross_masks[:1]
    first.step()
    block_parts = layout.return_rows(block_parts)
    dq, *dkv = attend_back(*operands, cross_masks[1], 0, count)
    operands, first.values, block_parts, dq, dkv = join(operands, first.values, block_parts, dq, dkv)
    cross_grads, cross_share = [dq], list(layout.return_share(dkv))
    first.step()
    dq, *dkv = attend_back(*operands, cross_masks[1], count, count)
    first.values, dq, dkv, cross_share = join(first.values, dq, dkv, cross_share)
    cross_grads.append(dq)
    cross_share += layout.return_share(dkv)
    first.step()
    grad_after_self, grad_self_heads, grad_w_pair, sums2 = run(
        functools.partial(after_self_back_kernel, calls),
        "after_self_back",
        tuple(cross_grads) + (after_self, normed2, self_low, grad_after_cross, norm2_gain, w_cross_q, w_out),
        (full_row, row, shaped((features, 2 * features)), sums),
        4 * unit,
    )
    cross_share, first.values, grad_w_pair = join(cross_share, first.values, grad_w_pair)
    first.step()
    grad_w_part, *memory_parts = run(
        functools.partial(memory_back_kernel, calls, layout.share),
        "memory_back",
        tuple(cross_share) + (memory_row, w_cross_kv, grad_w_cross_out, grad_w_pair),
        (shaped((features, 5 * features)),) + row_parts,
        4 * unit,
    )
    middle = Sum(layout, grad_w_part)

    operands = (queries, qmask, grad_self_heads, self_low, self_lse, keyvals)
    operands, middle.values, memory_parts, first.values = join(operands, middle.values, memory_parts, first.values)
    memory_parts = layout.return_rows(memory_parts)
    first.step()
    middle.step()
    dq, *dkv = attend_back(*operands, *self_masks, 0, count)
    operands, first.values, middle.values, memory_parts, dq, dkv = join(
        operands, first.values, middle.values, memory_parts, dq, dkv
    )
    self_grads, self_share = [dq], list(layout.return_share(dkv))
    first.step()
    middle.step()
    dq, *dkv = attend_back(*operands, *self_masks, count, count)
    first.values, middle.values, dq, dkv, self_share = join(first.values, middle.values, dq, dkv, self_share)
    self_grads.append(dq)
    self_share += layout.return_share(dkv)
    extra_rows = -(-(7 * features + hidden) // (16 * 3 * features)) * 16
    grad_w_qkv, small, *target_parts = run(
        functools.partial(project_back_kernel, calls, layout.share),
        "project_back",
        tuple(self_grads)
        + tuple(self_share)
        + (x, normed1, norm1_gain, w_qkv, grad_after_self, sums2, sums3, grad_b_up),
        (shaped((features, 3 * features)), shaped((extra_rows, 3 * features))) + row_parts,
        6 * unit,
    )
    last = Sum(layout, grad_w_qkv, small)
    last.step()
    last.values, first.values = join(last.values, first.values)
    grad_w_up, grad_w_down = unpack_feed(layout.place, first.values, hidden, features)
    last.step()
    last.values, grad_w_up, grad_w_down, block_parts = join(last.values, grad_w_up, grad_w_down, block_parts)
    last.values = jnp.concatenate([middle.values, last.values], 1)
    last.extra = jnp.pad(last.extra, ((0, 0), (0, middle.values.shape[1])))
    last.step()
    block_out = place_rows(layout.row, block_parts)
    last.values, block_out, memory_parts, target_parts = join(last.values, block_out, memory_parts, target_parts)
    last.step()
    memory_grad = place_rows(layout.row, memory_parts)
    last.values, memory_grad, target_parts = join(last.values, memory_grad, target_parts)
    target_parts = layout.return_rows(target_parts)
    last.step()
    last.values, target_parts = join(last.values, target_parts)
    last.step()
    target_grad = place_rows(layout.row, target_parts)
    grad_w_cross_out, grad_w_cross_q, grad_w_out, grad_w_cross_kv, grad_w_qkv = unpack_columns(
        layout.place, last.values, [features, features, features, 2 * features, 3 * features]
    )
    small = last.extra[:, : 3 * features].reshape(-1)[: 7 * features + hidden].astype(f32)
    (
        grad_norm1_gain,
        grad_norm1_bias,
        grad_norm2_gain,
        grad_norm2_bias,
        grad_norm3_gain,
        grad_norm3_bias,
        grad_b_down,
    ) = [small[i * features : (i + 1) * features] for i in range(7)]
    grad_b_up = small[7 * features :]
    return (
        block_out,
        target_grad,
        memory_grad,
        grad_norm1_gain,
        grad_norm1_bias,
        grad_w_qkv,
        grad_w_out,
        grad_norm2_gain,
        grad_norm2_bias,
        grad_w_cross_q,
        grad_w_cross_kv,
        grad_w_cross_out,
        grad_norm3_gain,
        grad_norm3_bias,
        grad_w_up,
        grad_b_up,
        grad_w_down,
        grad_b_down,
    )


def solution(mesh):
    token = P("dp", "blk", None)
    code = P("dp", "blk")
    return jax.shard_map(
        functools.partial(body, mesh.shape["dp"], mesh.shape["blk"]),
        mesh=mesh,
        in_specs=(token, token, code, code, code, code, token) + (P(),) * 15,
        out_specs=(token, token, token) + (P(),) * 15,
        check_vma=False,
    )
```

time: 598 us -> 430 us (0.72)
  Pallas kernels: 137 us -> 236 us
  matrix products: 73.2 us -> 0 us
  waiting for transfers between devices: 153 us -> 79.8 us
  blocking collectives: 48.7 us -> 0 us
  local copies, waits for them, and re-layouts: 63.4 us -> 18.5 us
  other arithmetic: 54 us -> 10.3 us
  starting transfers between devices: 47.7 us -> 74.8 us
  between operations: 15.5 us -> 1.69 us
    psum x1 -> x0, waiting for transfers between devices: 122 us -> none  [total_low(): sums = lax.psum(tuple((grad.astype(bf16) for grad in grads)), everywhere)]
    pallas_call x4 -> x20, Pallas kernels: 137 us -> 236 us  [the longest x4 93.9 us: attend_back(): pl.pallas_call(functools.partial(backward_kernel, parts), grid=(count,),...]
    dot_general x22 -> x0, matrix products: 73.2 us -> none  [dot(): return lax.dot_general(left, right, dims, preferred_element_type=f32)]
    ppermute x26 -> x56, waiting for transfers between devices: 30.3 us -> 79.8 us  [the longest x17 28.3 us: scatter(): arrived.append(lax.ppermute(send, axis, shift(step)))]
    psum x1 -> x0, blocking collectives: 48.7 us -> none  [body(): lax.psum((grad_norm1_gain, grad_norm1_bias, grad_norm2_gain, grad_norm2_b...]
    ppermute x26 -> x56, starting transfers between devices: 47.7 us -> 74.8 us  [the longest x9 21.2 us: bring_rows(): lax.ppermute(parts[step], 'blk', self.shift_rows(step))]
    reduce_sum x11 -> x0, other arithmetic: 13.4 us -> none  [the longest x5 9.66 us: layer_norm(): return centered * lax.rsqrt(spread + 1e-05) * scale_gain + shift_bias]
    convert_element_type x11 -> x12, other arithmetic: 22.1 us -> 9.37 us  [the longest x8 9.29 us: scatter(): self.values = total.astype(bf16)]
  transfers between devices with their start and end apart: 27 -> 56, of which waited for: 4 -> 16; matrix products, arithmetic and copies ran while one was open for 19% -> 4% of each run, Pallas kernels for 16% -> 43%
where the time goes in v2:
time: 430 us; the launch traced here: 421 us
  Pallas kernels  236 us (55%)
  waiting for transfers between devices  79.8 us (19%)
  starting transfers between devices  74.8 us (17%)
  local copies, waits for them, and re-layouts  18.5 us (4%)
  other arithmetic  10.3 us (2%)
    pallas_call x4, Pallas kernels, attend_back(): pl.pallas_call(functools.partial(backward_kernel, parts), grid=(count,),...  93.9 us
    pallas_call x2, Pallas kernels, attend(): pl.pallas_call(functools.partial(forward_kernel, parts), grid=(pairs,), i...  48.2 us
    pallas_call x6, Pallas kernels, run(): pl.pallas_call(kernel, grid=(1,), in_specs=specs, out_specs=[whole(out) f...  39.1 us
    ppermute x17, waiting for transfers between devices, scatter(): arrived.append(lax.ppermute(send, axis, shift(step)))  28.3 us
    pallas_call x1, Pallas kernels, feed_forward(): pl.pallas_call(functools.partial(feed_kernel, parts, share, each), grid_s...  27.9 us
    ppermute x9, starting transfers between devices, bring_rows(): lax.ppermute(parts[step], 'blk', self.shift_rows(step))  21.2 us
    ppermute x14, starting transfers between devices, gather(): lax.ppermute(mine, axis, shift(step))  18.7 us
    ppermute x17, starting transfers between devices, scatter(): arrived.append(lax.ppermute(send, axis, shift(step)))  18.5 us
  transfers between devices with their start and end apart: 56, of which 16 were waited for; matrix products, arithmetic and copies ran while one was open for 4% of the time, Pallas kernels for 43%

profile of v2, /device:TPU:0, one launch (start us, length us, event | category | flops | bytes accessed | tf_op | source)
XLA Modules:
  0.0 421.5 jit_solution(856116821104734877)
XLA Ops:
  0.7 2.2 pack_target.1
  2.9 3.0 collective-permute-start
  5.9 2.6 collective-permute-start.1
  9.9 2.8 pack_rows.1
  12.7 3.1 collective-permute-done.refs_1_
  15.8 11.1 %collective-permute-done.1.refs_2_ = bf16[272,512]{1,0:T(8,128)(2,1)S(1)} collective-permute-done((bf16[272,512]{1,0:T(8,128)(2,1)}, bf16[272,512]{1,0:T(8,128)(2,1)S(1)}, u32[]{:S(2)}, u32[]{:S(2)}) %collective-permute-start.1) | collective-permute-done | bytes 278560 | tf_op jit(solution)/shard_map/ppermute | solution.py:623
  27.7 5.7 %project.1 = (bf16[1024,512]{1,0:T(8,128)(2,1)}, bf16[1024,512]{1,0:T(8,128)(2,1)}, bf16[1024,512]{1,0:T(8,128)(2,1)}, bf16[1024,1280]{1,0:T(8,128)(2,1)}, bf16[1024,128]{1,0:T(8,128)(2,1)}) custom-call(bf16[272,512]{1,0:T(8,128)(2,1)} %get-tuple-element.212.refs_0_, bf16[272,512]{1,0:T(8,128)(2,1)} %copy-done.19, bf16[272,512]{1,0:T(8,128)(2,1)} %copy-done.20, ...), custom_call_target="tpu_custom_call" | custom-call | flops 1610612736 | bytes 8720384 | tf_op jit(solution)/shard_map/project/pallas_call | solution.py:64
  33.4 6.4 %collective-permute-start.4 = (bf16[256,512]{1,0:T(8,128)(2,1)S(1)}, bf16[256,512]{1,0:T(8,128)(2,1)S(1)}, u32[]{:S(2)}, u32[]{:S(2)}) collective-permute-start(bf16[256,512]{1,0:T(8,128)(2,1)S(1)} %copy-done.32), channel_id=1, source_target_pairs={{0,2},{1,3},{2,4},{3,5},{4,6},{5,7},{6,0},{7,1},{8,10},{9,11},{10,... | collective-permute-start | bytes 786440 | tf_op jit(solution)/shard_map/ppermute | solution.py:623
  43.8 24.1 %attend.2 = (bf16[1024,512]{1,0:T(8,128)(2,1)}, f32[4,2,1024]{2,1,0:T(2,128)}) custom-call(bf16[1024,512]{1,0:T(8,128)(2,1)} %get-tuple-element.328.refs_0_, bf16[1024,128]{1,0:T(8,128)(2,1)} %get-tuple-element.329.refs_1_, bf16[1024,1280]{1,0:T(8,128)(2,1)} %get-tuple-element.333.refs_2_.refs_4_.refs_6_.refs_9_.refs_5_.refs_7_, ...), custom_call_target="tpu_custom_call" | custom-call | flops 8589934592 | bytes 6291456 | tf_op jit(solution)/shard_map/attend/pallas_call | solution.py:110
  68.7 4.1 memory.1
  72.9 4.7 %after_self.1 = (f32[1024,512]{1,0:T(8,128)}, bf16[1024,512]{1,0:T(8,128)(2,1)}, bf16[1024,512]{1,0:T(8,128)(2,1)}) custom-call(bf16[1024,512]{1,0:T(8,128)(2,1)} %get-tuple-element.218.x_ref.refs_6_, bf16[1024,512]{1,0:T(8,128)(2,1)} %get-tuple-element.331.attended_ref.refs_4_.refs_3_, bf16[512,512]{1,0:T(8,128)(2,1)} %refs_8_.1, f32[1,512]{1,0:T(1,128)} %bitcast.10, ...), custom_call_target="tpu_custom_call" | custom-call | flops 1073741824 | bytes 7344128 | tf_op jit(solution)/shard_map/after_self/pallas_call | solution.py:64
  77.6 2.8 collective-permute-start.8
  83.1 24.1 %attend.3 = (bf16[1024,512]{1,0:T(8,128)(2,1)}, f32[4,2,1024]{2,1,0:T(2,128)}) custom-call(bf16[1024,512]{1,0:T(8,128)(2,1)} %get-tuple-element.272.refs_0_, bf16[1024,128]{1,0:T(8,128)(2,1)} %get-tuple-element.329.refs_1_, bf16[1024,1024]{1,0:T(8,128)(2,1)} %get-tuple-element.277.refs_2_.refs_4_.refs_5_.refs_7_, bf16[1024,1024]{1,0:T(8,128)(2,1)} %copy-done.16, ...), custom_call_target="tpu_custom_call" | custom-call | flops 8589934592 | bytes 6291456 | tf_op jit(solution)/shard_map/attend/pallas_call | solution.py:110
  108.1 27.9 %feed_forward.1 = (bf16[256,512]{1,0:T(8,128)(2,1)}, bf16[256,512]{1,0:T(8,128)(2,1)}, bf16[256,512]{1,0:T(8,128)(2,1)}, bf16[256,512]{1,0:T(8,128)(2,1)}, bf16[...) custom-call(s32[1]{0:T(128)} %bitcast.5.place_ref, ...), custom_call_target="tpu_custom_call" | custom-call | flops 14495514624 | bytes 23068672 | tf_op jit(solution)/shard_map/feed_forward/pallas_call | solution.py:478
  138.9 23.7 %attend_back.4 = (bf16[1024,256]{1,0:T(8,128)(2,1)}, bf16[1024,512]{1,0:T(8,128)(2,1)}, bf16[1024,512]{1,0:T(8,128)(2,1)}) custom-call(bf16[1024,512]{1,0:T(8,128)(2,1)} %get-tuple-element.272.refs_0_, bf16[1024,128]{1,0:T(8,128)(2,1)} %get-tuple-element.329.refs_1_, bf16[1024,512]{1,0:T(8,128)(2,1)} %get-tuple-element.274.refs_2_, ...), custom_call_target="tpu_custom_call" | custom-call | flops 10737418240 | bytes 6291456 | tf_op jit(solution)/shard_map/attend_back/pallas_call | solution.py:172
  164.0 2.8 add_convert_fusion
  167.8 2.5 collective-permute-start.17
  171.4 23.5 %attend_back.5 = (bf16[1024,256]{1,0:T(8,128)(2,1)}, bf16[1024,512]{1,0:T(8,128)(2,1)}, bf16[1024,512]{1,0:T(8,128)(2,1)}) custom-call(bf16[1024,512]{1,0:T(8,128)(2,1)} %get-tuple-element.272.refs_0_, bf16[1024,128]{1,0:T(8,128)(2,1)} %get-tuple-element.329.refs_1_, bf16[1024,512]{1,0:T(8,128)(2,1)} %get-tuple-element.274.refs_2_, ...), custom_call_target="tpu_custom_call" | custom-call | flops 10737418240 | bytes 6291456 | tf_op jit(solution)/shard_map/attend_back/pallas_call | solution.py:172
  197.2 3.8 collective-permute-start.22
  201.6 7.5 %after_self_back.1 = (f32[1024,512]{1,0:T(8,128)}, bf16[1024,512]{1,0:T(8,128)(2,1)}, bf16[512,1024]{1,0:T(8,128)(2,1)}, f32[8,512]{1,0:T(8,128)}) custom-call(bf16[1024,256]{1,0:T(8,128)(2,1)} %get-tuple-element.270.refs_0_, bf16[1024,256]{1,0:T(8,128)(2,1)} %get-tuple-element.286.refs_1_, f32[1024,512]{1,0:T(8,128)} %get-tuple-element.246.refs_0_.refs_2_, ...), custom_call_target="tpu_custom_call" | custom-call | flops 2147483648 | bytes 12601344 | tf_op jit(solution)/shard_map/after_self_back/pallas_call | solution.py:64
  209.1 4.1 collective-permute-done.21
  215.3 2.8 collective-permute-start.25
  218.1 7.2 %memory_back.1 = (bf16[512,2560]{1,0:T(8,128)(2,1)}, bf16[256,512]{1,0:T(8,128)(2,1)}, bf16[256,512]{1,0:T(8,128)(2,1)}, bf16[256,512]{1,0:T(8,128)(2,1)}, bf16[256,512]{1,0:T(8,128)(2,1)}) custom-call(bf16[1024,512]{1,0:T(8,128)(2,1)} %get-tuple-element.297.refs_0_, bf16[1024,512]{1,0:T(8,128)(2,1)} %collective-permute-done.18.refs_1_, ...), custom_call_target="tpu_custom_call" | custom-call | flops 2147483648 | bytes 11534336 | tf_op jit(solution)/shard_map/memory_back/pallas_call | solution.py:64
  226.0 2.5 collective-permute-start.26
  231.5 3.7 collective-permute-start.30
  235.1 23.3 %attend_back.6 = (bf16[1024,256]{1,0:T(8,128)(2,1)}, bf16[1024,512]{1,0:T(8,128)(2,1)}, bf16[1024,512]{1,0:T(8,128)(2,1)}) custom-call(bf16[1024,512]{1,0:T(8,128)(2,1)} %get-tuple-element.328.refs_0_, bf16[1024,128]{1,0:T(8,128)(2,1)} %get-tuple-element.329.refs_1_, bf16[1024,512]{1,0:T(8,128)(2,1)} %get-tuple-element.330.refs_2_, ...), custom_call_target="tpu_custom_call" | custom-call | flops 10737418240 | bytes 6291456 | tf_op jit(solution)/shard_map/attend_back/pallas_call | solution.py:172
  263.3 2.4 add_convert_fusion.1
  265.8 12.8 %collective-permute-done.31.refs_2_ = bf16[256,512]{1,0:T(8,128)(2,1)S(1)} collective-permute-done((bf16[256,512]{1,0:T(8,128)(2,1)S(1)}, bf16[256,512]{1,0:T(8,128)(2,1)S(1)}, u32[]{:S(2)}, u32[]{:S(2)}) %collective-permute-start.31) | collective-permute-done | bytes 262176 | tf_op jit(solution)/shard_map/ppermute | solution.py:628
  283.9 23.5 %attend_back.7 = (bf16[1024,256]{1,0:T(8,128)(2,1)}, bf16[1024,512]{1,0:T(8,128)(2,1)}, bf16[1024,512]{1,0:T(8,128)(2,1)}) custom-call(bf16[1024,512]{1,0:T(8,128)(2,1)} %get-tuple-element.328.refs_0_, bf16[1024,128]{1,0:T(8,128)(2,1)} %get-tuple-element.329.refs_1_, bf16[1024,512]{1,0:T(8,128)(2,1)} %get-tuple-element.330.refs_2_, ...), custom_call_target="tpu_custom_call" | custom-call | flops 10737418240 | bytes 6291456 | tf_op jit(solution)/shard_map/attend_back/pallas_call | solution.py:172
  309.8 2.5 collective-permute-done.38.refs_5_
  313.3 9.8 %project_back.1 = (bf16[512,1536]{1,0:T(8,128)(2,1)}, bf16[16,1536]{1,0:T(8,128)(2,1)}, bf16[256,512]{1,0:T(8,128)(2,1)}, bf16[256,512]{1,0:T(8,128)(2,1)}, bf16...) custom-call(bf16[1024,256]{1,0:T(8,128)(2,1)} %get-tuple-element.341.refs_0_, ...), custom_call_target="tpu_custom_call" | custom-call | flops 3221225472 | bytes 13723648 | tf_op jit(solution)/shard_map/project_back/pallas_call | solution.py:64
  328.1 2.4 collective-permute-start.42
  332.1 7.0 %unpack_feed.1 = (f32[512,2048]{1,0:T(8,128)}, f32[2048,512]{1,0:T(8,128)}) custom-call(s32[1]{0:T(128)} %bitcast.5.place_ref, bf16[2048,512]{1,0:T(8,128)(2,1)} %copy-done.1, bf16[2048,512]{1,0:T(8,128)(2,1)} %collective-permute-done.33.refs_1_), custom_call_target="tpu_custom_call" | custom-call | tf_op jit(solution)/shard_map/unpack_feed/pallas_call | solution.py:332
  339.1 4.6 %collective-permute-done.41 = bf16[80,1536]{1,0:T(8,128)(2,1)S(1)} collective-permute-done((bf16[80,1536]{1,0:T(8,128)(2,1)S(1)}, bf16[80,1536]{1,0:T(8,128)(2,1)S(1)}, u32[]{:S(2)}, u32[]{:S(2)}) %collective-permute-start.41) | collective-permute-done | bytes 245792 | tf_op jit(solution)/shard_map/ppermute | solution.py:677
  346.7 3.0 place_rows.3
  349.7 3.0 collective-permute-done.45
  352.7 14.5 %collective-permute-done.44 = bf16[32,4096]{1,0:T(8,128)(2,1)S(1)} collective-permute-done((bf16[32,4096]{1,0:T(8,128)(2,1)S(1)}, bf16[32,4096]{1,0:T(8,128)(2,1)S(1)}, u32[]{:S(2)}, u32[]{:S(2)}) %collective-permute-start.44) | collective-permute-done | bytes 262176 | tf_op jit(solution)/shard_map/ppermute | solution.py:677
  369.8 2.8 collective-permute-start.48
  372.7 3.1 place_rows.4
  375.9 3.5 collective-permute-done.47
  381.6 2.3 collective-permute-start.51
  384.2 5.2 %collective-permute-start.52 = (bf16[256,512]{1,0:T(8,128)(2,1)S(1)}, bf16[256,512]{1,0:T(8,128)(2,1)S(1)}, u32[]{:S(2)}, u32[]{:S(2)}) collective-permute-start(bf16[256,512]{1,0:T(8,128)(2,1)S(1)} %copy-done.24), channel_id=1, source_target_pairs={{0,6},{1,7},{2,0},{3,1},{4,2},{5,3},{6,4},{7,5},{8,14},{9,15},{10,... | collective-permute-start | bytes 786440 | tf_op jit(solution)/shard_map/ppermute | solution.py:628
  389.4 5.8 %collective-permute-done.49 = bf16[64,4096]{1,0:T(8,128)(2,1)S(1)} collective-permute-done((bf16[64,4096]{1,0:T(8,128)(2,1)S(1)}, bf16[64,4096]{1,0:T(8,128)(2,1)S(1)}, u32[]{:S(2)}, u32[]{:S(2)}) %collective-permute-start.49) | collective-permute-done | bytes 524320 | tf_op jit(solution)/shard_map/ppermute | solution.py:689
  395.2 2.8 collective-permute-start.54
  398.1 6.3 %collective-permute-done.50 = bf16[64,4096]{1,0:T(8,128)(2,1)S(1)} collective-permute-done((bf16[64,4096]{1,0:T(8,128)(2,1)S(1)}, bf16[64,4096]{1,0:T(8,128)(2,1)S(1)}, u32[]{:S(2)}, u32[]{:S(2)}) %collective-permute-start.50) | collective-permute-done | bytes 524320 | tf_op jit(solution)/shard_map/ppermute | solution.py:689
  404.6 5.7 %collective-permute-done.53.refs_2_ = bf16[256,512]{1,0:T(8,128)(2,1)S(1)} collective-permute-done((bf16[256,512]{1,0:T(8,128)(2,1)S(1)}, bf16[256,512]{1,0:T(8,128)(2,1)S(1)}, u32[]{:S(2)}, u32[]{:S(2)}) %collective-permute-start.53) | collective-permute-done | bytes 262176 | tf_op jit(solution)/shard_map/ppermute | solution.py:628
  412.4 3.0 place_rows.5
  415.4 5.9 %unpack_columns.1 = (f32[512,512]{1,0:T(8,128)}, f32[512,512]{1,0:T(8,128)}, f32[512,512]{1,0:T(8,128)}, f32[512,1024]{1,0:T(8,128)}, f32[512,1536]{1,0:T(8,128)}) custom-call(s32[1]{0:T(128)} %bitcast.5.place_ref, bf16[256,4096]{1,0:T(8,128)(2,1)} %copy-done, bf16[256,4096]{1,0:T(8,128)(2,1)} %collective-permute-done.55.refs_1_), custom_call_target="tpu_custom_call" | custom-call | tf_op jit(solution)/shard_map/unpack_columns/pallas_call | solution.py:363
  (211 shorter events, 55.7 us)
Async XLA Ops:
  2.9 12.9 %collective-permute-start = (bf16[272,512]{1,0:T(8,128)(2,1)}, bf16[272,512]{1,0:T(8,128)(2,1)S(1)}, u32[]{:S(2)}, u32[]{:S(2)}) collective-permute-start(bf16[272,512]{1,0:T(8,128)(2,1)} %get-tuple-element.213), channel_id=1, source_target_pairs={{0,2},{1,3},{2,4},{3,5},{4,6},{5,7},{6,0},{7,1},{8,10},{9,11},{10,... | collective-permute-start | bytes 835592 | tf_op jit(solution)/shard_map/ppermute | solution.py:623
  5.9 21.0 %collective-permute-start.1 = (bf16[272,512]{1,0:T(8,128)(2,1)}, bf16[272,512]{1,0:T(8,128)(2,1)S(1)}, u32[]{:S(2)}, u32[]{:S(2)}) collective-permute-start(bf16[272,512]{1,0:T(8,128)(2,1)} %get-tuple-element.214), channel_id=1, source_target_pairs={{0,4},{1,5},{2,6},{3,7},{4,0},{5,1},{6,2},{7,3},{8,12},{9,13},{10,... | collective-permute-start | bytes 835592 | tf_op jit(solution)/shard_map/ppermute | solution.py:623
  8.5 18.4 %collective-permute-start.2 = (bf16[272,512]{1,0:T(8,128)(2,1)}, bf16[272,512]{1,0:T(8,128)(2,1)S(1)}, u32[]{:S(2)}, u32[]{:S(2)}) collective-permute-start(bf16[272,512]{1,0:T(8,128)(2,1)} %get-tuple-element.215), channel_id=1, source_target_pairs={{0,6},{1,7},{2,0},{3,1},{4,2},{5,3},{6,4},{7,5},{8,14},{9,15},{10,... | collective-permute-start | bytes 835592 | tf_op jit(solution)/shard_map/ppermute | solution.py:623
  33.4 34.5 %collective-permute-start.4 = (bf16[256,512]{1,0:T(8,128)(2,1)S(1)}, bf16[256,512]{1,0:T(8,128)(2,1)S(1)}, u32[]{:S(2)}, u32[]{:S(2)}) collective-permute-start(bf16[256,512]{1,0:T(8,128)(2,1)S(1)} %copy-done.32), channel_id=1, source_target_pairs={{0,2},{1,3},{2,4},{3,5},{4,6},{5,7},{6,0},{7,1},{8,10},{9,11},{10,... | collective-permute-start | bytes 786440 | tf_op jit(solution)/shard_map/ppermute | solution.py:623
  39.8 28.1 %collective-permute-start.5 = (bf16[256,512]{1,0:T(8,128)(2,1)S(1)}, bf16[256,512]{1,0:T(8,128)(2,1)S(1)}, u32[]{:S(2)}, u32[]{:S(2)}) collective-permute-start(bf16[256,512]{1,0:T(8,128)(2,1)S(1)} %copy-done.31), channel_id=1, source_target_pairs={{0,4},{1,5},{2,6},{3,7},{4,0},{5,1},{6,2},{7,3},{8,12},{9,13},{10,... | collective-permute-start | bytes 786440 | tf_op jit(solution)/shard_map/ppermute | solution.py:623
  41.5 26.4 %collective-permute-start.6 = (bf16[256,512]{1,0:T(8,128)(2,1)S(1)}, bf16[256,512]{1,0:T(8,128)(2,1)}, u32[]{:S(2)}, u32[]{:S(2)}) collective-permute-start(bf16[256,512]{1,0:T(8,128)(2,1)S(1)} %copy-done.30), channel_id=1, source_target_pairs={{0,6},{1,7},{2,0},{3,1},{4,2},{5,3},{6,4},{7,5},{8,14},{9,15},{10,... | collective-permute-start | bytes 786440 | tf_op jit(solution)/shard_map/ppermute | solution.py:623
  77.6 29.6 %collective-permute-start.8 = (bf16[256,512]{1,0:T(8,128)(2,1)S(1)}, bf16[256,512]{1,0:T(8,128)(2,1)S(1)}, u32[]{:S(2)}, u32[]{:S(2)}) collective-permute-start(bf16[256,512]{1,0:T(8,128)(2,1)S(1)} %copy-done.29), channel_id=1, source_target_pairs={{0,2},{1,3},{2,4},{3,5},{4,6},{5,7},{6,0},{7,1},{8,10},{9,11},{10,... | collective-permute-start | bytes 786440 | tf_op jit(solution)/shard_map/ppermute | solution.py:623
  80.4 26.8 %collective-permute-start.9 = (bf16[256,512]{1,0:T(8,128)(2,1)S(1)}, bf16[256,512]{1,0:T(8,128)(2,1)S(1)}, u32[]{:S(2)}, u32[]{:S(2)}) collective-permute-start(bf16[256,512]{1,0:T(8,128)(2,1)S(1)} %copy-done.28), channel_id=1, source_target_pairs={{0,4},{1,5},{2,6},{3,7},{4,0},{5,1},{6,2},{7,3},{8,12},{9,13},{10,... | collective-permute-start | bytes 786440 | tf_op jit(solution)/shard_map/ppermute | solution.py:623
  82.1 25.2 %collective-permute-start.10 = (bf16[256,512]{1,0:T(8,128)(2,1)S(1)}, bf16[256,512]{1,0:T(8,128)(2,1)S(1)}, u32[]{:S(2)}, u32[]{:S(2)}) collective-permute-start(bf16[256,512]{1,0:T(8,128)(2,1)S(1)} %copy-done.27), channel_id=1, source_target_pairs={{0,6},{1,7},{2,0},{3,1},{4,2},{5,3},{6,4},{7,5},{8,14},{9,15},{10,... | collective-permute-start | bytes 786440 | tf_op jit(solution)/shard_map/ppermute | solution.py:623
  136.0 26.7 %collective-permute-start.11 = (bf16[2048,512]{1,0:T(8,128)(2,1)}, bf16[2048,512]{1,0:T(8,128)(2,1)S(1)}, u32[]{:S(2)}, u32[]{:S(2)}) collective-permute-start(bf16[2048,512]{1,0:T(8,128)(2,1)} %get-tuple-element.262), channel_id=1, source_target_pairs={{0,1},{1,0},{2,3},{3,2},{4,5},{5,4},{6,7},{7,6},{8,9},{9,8},{10,11... | collective-permute-start | bytes 6291464 | tf_op jit(solution)/shard_map/ppermute | solution.py:662
  136.1 30.7 %collective-permute-start.12 = (bf16[256,512]{1,0:T(8,128)(2,1)}, bf16[256,512]{1,0:T(8,128)(2,1)S(1)}, u32[]{:S(2)}, u32[]{:S(2)}) collective-permute-start(bf16[256,512]{1,0:T(8,128)(2,1)} %get-tuple-element.264), channel_id=1, source_target_pairs={{0,6},{1,7},{2,0},{3,1},{4,2},{5,3},{6,4},{7,5},{8,14},{9,15},{10,... | collective-permute-start | bytes 786440 | tf_op jit(solution)/shard_map/ppermute | solution.py:628
  138.1 28.7 %collective-permute-start.13 = (bf16[256,512]{1,0:T(8,128)(2,1)}, bf16[256,512]{1,0:T(8,128)(2,1)S(1)}, u32[]{:S(2)}, u32[]{:S(2)}) collective-permute-start(bf16[256,512]{1,0:T(8,128)(2,1)} %get-tuple-element.265), channel_id=1, source_target_pairs={{0,4},{1,5},{2,6},{3,7},{4,0},{5,1},{6,2},{7,3},{8,12},{9,13},{10,... | collective-permute-start | bytes 786440 | tf_op jit(solution)/shard_map/ppermute | solution.py:628
  138.8 28.0 %collective-permute-start.14 = (bf16[256,512]{1,0:T(8,128)(2,1)}, bf16[256,512]{1,0:T(8,128)(2,1)S(1)}, u32[]{:S(2)}, u32[]{:S(2)}) collective-permute-start(bf16[256,512]{1,0:T(8,128)(2,1)} %get-tuple-element.266), channel_id=1, source_target_pairs={{0,2},{1,3},{2,4},{3,5},{4,6},{5,7},{6,0},{7,1},{8,10},{9,11},{10,... | collective-permute-start | bytes 786440 | tf_op jit(solution)/shard_map/ppermute | solution.py:628
  167.8 27.1 %collective-permute-start.17 = (bf16[512,512]{1,0:T(8,128)(2,1)S(1)}, bf16[512,512]{1,0:T(8,128)(2,1)}, u32[]{:S(2)}, u32[]{:S(2)}) collective-permute-start(bf16[512,512]{1,0:T(8,128)(2,1)S(1)} %get-tuple-element.407), channel_id=1, source_target_pairs={{0,24},{8,0},{16,8},{24,16},{1,25},{9,1},{17,9},{25,17},{2,26},{10... | collective-permute-start | bytes 1572872 | tf_op jit(solution)/shard_map/ppermute | solution.py:677
  170.3 24.7 %collective-permute-start.16 = (bf16[512,512]{1,0:T(8,128)(2,1)S(1)}, bf16[512,512]{1,0:T(8,128)(2,1)}, u32[]{:S(2)}, u32[]{:S(2)}) collective-permute-start(bf16[512,512]{1,0:T(8,128)(2,1)S(1)} %get-tuple-element.408), channel_id=1, source_target_pairs={{0,16},{8,24},{16,0},{24,8},{1,17},{9,25},{17,1},{25,9},{2,18},{10... | collective-permute-start | bytes 1572872 | tf_op jit(solution)/shard_map/ppermute | solution.py:677
  170.8 24.2 %collective-permute-start.15 = (bf16[512,512]{1,0:T(8,128)(2,1)S(1)}, bf16[512,512]{1,0:T(8,128)(2,1)}, u32[]{:S(2)}, u32[]{:S(2)}) collective-permute-start(bf16[512,512]{1,0:T(8,128)(2,1)S(1)} %get-tuple-element.406), channel_id=1, source_target_pairs={{0,8},{8,16},{16,24},{24,0},{1,9},{9,17},{17,25},{25,1},{2,10},{10... | collective-permute-start | bytes 1572872 | tf_op jit(solution)/shard_map/ppermute | solution.py:677
  171.4 25.2 %collective-permute-start.18 = (bf16[1024,512]{1,0:T(8,128)(2,1)}, bf16[1024,512]{1,0:T(8,128)(2,1)}, u32[]{:S(2)}, u32[]{:S(2)}) collective-permute-start(bf16[1024,512]{1,0:T(8,128)(2,1)} %get-tuple-element.285), channel_id=1, source_target_pairs={{0,1},{1,0},{2,3},{3,2},{4,5},{5,4},{6,7},{7,6},{8,9},{9,8},{10,11... | collective-permute-start | bytes 3145736 | tf_op jit(solution)/shard_map/ppermute | solution.py:638
  196.6 16.7 %collective-permute-start.19 = (bf16[1024,512]{1,0:T(8,128)(2,1)}, bf16[1024,512]{1,0:T(8,128)(2,1)S(1)}, u32[]{:S(2)}, u32[]{:S(2)}) collective-permute-start(bf16[1024,512]{1,0:T(8,128)(2,1)} %get-tuple-element.294), channel_id=1, source_target_pairs={{0,1},{1,0},{2,3},{3,2},{4,5},{5,4},{6,7},{7,6},{8,9},{9,8},{10,11... | collective-permute-start | bytes 3145736 | tf_op jit(solution)/shard_map/ppermute | solution.py:638
  197.2 11.9 %collective-permute-start.22 = (bf16[128,512]{1,0:T(8,128)(2,1)S(1)}, bf16[128,512]{1,0:T(8,128)(2,1)S(1)}, u32[]{:S(2)}, u32[]{:S(2)}) collective-permute-start(bf16[128,512]{1,0:T(8,128)(2,1)S(1)} %get-tuple-element.419), channel_id=1, source_target_pairs={{0,6},{1,7},{2,0},{3,1},{4,2},{5,3},{6,4},{7,5},{8,14},{9,15},{10,... | collective-permute-start | bytes 393224 | tf_op jit(solution)/shard_map/ppermute | solution.py:677
  201.0 12.2 %collective-permute-start.21 = (bf16[128,512]{1,0:T(8,128)(2,1)S(1)}, bf16[128,512]{1,0:T(8,128)(2,1)S(1)}, u32[]{:S(2)}, u32[]{:S(2)}) collective-permute-start(bf16[128,512]{1,0:T(8,128)(2,1)S(1)} %get-tuple-element.420), channel_id=1, source_target_pairs={{0,4},{1,5},{2,6},{3,7},{4,0},{5,1},{6,2},{7,3},{8,12},{9,13},{10,... | collective-permute-start | bytes 393224 | tf_op jit(solution)/shard_map/ppermute | solution.py:677
  201.3 11.9 %collective-permute-start.20 = (bf16[128,512]{1,0:T(8,128)(2,1)S(1)}, bf16[128,512]{1,0:T(8,128)(2,1)S(1)}, u32[]{:S(2)}, u32[]{:S(2)}) collective-permute-start(bf16[128,512]{1,0:T(8,128)(2,1)S(1)} %get-tuple-element.418), channel_id=1, source_target_pairs={{0,2},{1,3},{2,4},{3,5},{4,6},{5,7},{6,0},{7,1},{8,10},{9,11},{10,... | collective-permute-start | bytes 393224 | tf_op jit(solution)/shard_map/ppermute | solution.py:677
  213.3 12.0 %collective-permute-start.23 = (bf16[128,512]{1,0:T(8,128)(2,1)S(1)}, bf16[128,512]{1,0:T(8,128)(2,1)S(1)}, u32[]{:S(2)}, u32[]{:S(2)}) collective-permute-start(bf16[128,512]{1,0:T(8,128)(2,1)S(1)} %add_convert_fusion.7), channel_id=1, source_target_pairs={{0,2},{1,3},{2,4},{3,5},{4,6},{5,7},{6,0},{7,1},{8,10},{9,11},{10,... | collective-permute-start | bytes 393224 | tf_op jit(solution)/shard_map/ppermute | solution.py:689
  213.4 12.6 %collective-permute-start.24 = (bf16[128,512]{1,0:T(8,128)(2,1)S(1)}, bf16[128,512]{1,0:T(8,128)(2,1)S(1)}, u32[]{:S(2)}, u32[]{:S(2)}) collective-permute-start(bf16[128,512]{1,0:T(8,128)(2,1)S(1)} %add_convert_fusion.7), channel_id=1, source_target_pairs={{0,4},{1,5},{2,6},{3,7},{4,0},{5,1},{6,2},{7,3},{8,12},{9,13},{10,... | collective-permute-start | bytes 393224 | tf_op jit(solution)/shard_map/ppermute | solution.py:689
  215.3 10.7 %collective-permute-start.25 = (bf16[128,512]{1,0:T(8,128)(2,1)S(1)}, bf16[128,512]{1,0:T(8,128)(2,1)S(1)}, u32[]{:S(2)}, u32[]{:S(2)}) collective-permute-start(bf16[128,512]{1,0:T(8,128)(2,1)S(1)} %add_convert_fusion.7), channel_id=1, source_target_pairs={{0,6},{1,7},{2,0},{3,1},{4,2},{5,3},{6,4},{7,5},{8,14},{9,15},{10,... | collective-permute-start | bytes 393224 | tf_op jit(solution)/shard_map/ppermute | solution.py:689
  226.0 32.6 %collective-permute-start.26 = (bf16[512,512]{1,0:T(8,128)(2,1)S(1)}, bf16[512,512]{1,0:T(8,128)(2,1)}, u32[]{:S(2)}, u32[]{:S(2)}) collective-permute-start(bf16[512,512]{1,0:T(8,128)(2,1)S(1)} %constant_dynamic-update-slice_fusion.12), channel_id=1, source_target_pairs={{0,8},{8,16},{16,24},{24,0},{1,9},{9,17},{17,25},{25,1},{2,10},{10... | collective-permute-start | bytes 1572872 | tf_op jit(solution)/shard_map/ppermute | solution.py:689
  228.5 32.4 %collective-permute-start.27 = (bf16[512,512]{1,0:T(8,128)(2,1)S(1)}, bf16[512,512]{1,0:T(8,128)(2,1)}, u32[]{:S(2)}, u32[]{:S(2)}) collective-permute-start(bf16[512,512]{1,0:T(8,128)(2,1)S(1)} %constant_dynamic-update-slice_fusion.12), channel_id=1, source_target_pairs={{0,16},{8,24},{16,0},{24,8},{1,17},{9,25},{17,1},{25,9},{2,18},{10... | collective-permute-start | bytes 1572872 | tf_op jit(solution)/shard_map/ppermute | solution.py:689
  229.0 33.2 %collective-permute-start.28 = (bf16[512,512]{1,0:T(8,128)(2,1)S(1)}, bf16[512,512]{1,0:T(8,128)(2,1)}, u32[]{:S(2)}, u32[]{:S(2)}) collective-permute-start(bf16[512,512]{1,0:T(8,128)(2,1)S(1)} %constant_dynamic-update-slice_fusion.12), channel_id=1, source_target_pairs={{0,24},{8,0},{16,8},{24,16},{1,25},{9,1},{17,9},{25,17},{2,26},{10... | collective-permute-start | bytes 1572872 | tf_op jit(solution)/shard_map/ppermute | solution.py:689
  231.4 31.9 %collective-permute-start.29 = (bf16[256,2560]{1,0:T(8,128)(2,1)S(1)}, bf16[256,2560]{1,0:T(8,128)(2,1)}, u32[]{:S(2)}, u32[]{:S(2)}) collective-permute-start(bf16[256,2560]{1,0:T(8,128)(2,1)S(1)} %constant_dynamic-slice_fusion.10), channel_id=1, source_target_pairs={{0,1},{1,0},{2,3},{3,2},{4,5},{5,4},{6,7},{7,6},{8,9},{9,8},{10,11... | collective-permute-start | bytes 3932168 | tf_op jit(solution)/shard_map/ppermute | solution.py:677
  231.5 34.3 %collective-permute-start.30 = (bf16[256,512]{1,0:T(8,128)(2,1)}, bf16[256,512]{1,0:T(8,128)(2,1)}, u32[]{:S(2)}, u32[]{:S(2)}) collective-permute-start(bf16[256,512]{1,0:T(8,128)(2,1)} %get-tuple-element.320), channel_id=1, source_target_pairs={{0,6},{1,7},{2,0},{3,1},{4,2},{5,3},{6,4},{7,5},{8,14},{9,15},{10,... | collective-permute-start | bytes 786440 | tf_op jit(solution)/shard_map/ppermute | solution.py:628
  259.4 19.2 %collective-permute-start.31 = (bf16[256,512]{1,0:T(8,128)(2,1)S(1)}, bf16[256,512]{1,0:T(8,128)(2,1)S(1)}, u32[]{:S(2)}, u32[]{:S(2)}) collective-permute-start(bf16[256,512]{1,0:T(8,128)(2,1)S(1)} %copy-done.26), channel_id=1, source_target_pairs={{0,4},{1,5},{2,6},{3,7},{4,0},{5,1},{6,2},{7,3},{8,12},{9,13},{10,... | collective-permute-start | bytes 786440 | tf_op jit(solution)/shard_map/ppermute | solution.py:628
  260.9 17.7 %collective-permute-start.32 = (bf16[256,512]{1,0:T(8,128)(2,1)S(1)}, bf16[256,512]{1,0:T(8,128)(2,1)S(1)}, u32[]{:S(2)}, u32[]{:S(2)}) collective-permute-start(bf16[256,512]{1,0:T(8,128)(2,1)S(1)} %copy-done.25), channel_id=1, source_target_pairs={{0,2},{1,3},{2,4},{3,5},{4,6},{5,7},{6,0},{7,1},{8,10},{9,11},{10,... | collective-permute-start | bytes 786440 | tf_op jit(solution)/shard_map/ppermute | solution.py:628
  279.4 29.9 %collective-permute-start.33 = (bf16[2048,512]{1,0:T(8,128)(2,1)S(1)}, bf16[2048,512]{1,0:T(8,128)(2,1)}, u32[]{:S(2)}, u32[]{:S(2)}) collective-permute-start(bf16[2048,512]{1,0:T(8,128)(2,1)S(1)} %constant_dynamic-update-slice_fusion.8.refs_0_), channel_id=1, source_target_pairs={{0,1},{1,0},{2,3},{3,2},{4,5},{5,4},{6,7},{7,6},{8,9},{9,8},{10,11... | collective-permute-start | bytes 6291464 | tf_op jit(solution)/shard_map/ppermute | solution.py:689
  280.4 26.9 %collective-permute-start.36 = (bf16[64,2560]{1,0:T(8,128)(2,1)}, bf16[64,2560]{1,0:T(8,128)(2,1)S(1)}, u32[]{:S(2)}, u32[]{:S(2)}) collective-permute-start(bf16[64,2560]{1,0:T(8,128)(2,1)} %get-tuple-element.410), channel_id=1, source_target_pairs={{0,24},{8,0},{16,8},{24,16},{1,25},{9,1},{17,9},{25,17},{2,26},{10... | collective-permute-start | bytes 983048 | tf_op jit(solution)/shard_map/ppermute | solution.py:677
  282.4 24.9 %collective-permute-start.35 = (bf16[64,2560]{1,0:T(8,128)(2,1)}, bf16[64,2560]{1,0:T(8,128)(2,1)}, u32[]{:S(2)}, u32[]{:S(2)}) collective-permute-start(bf16[64,2560]{1,0:T(8,128)(2,1)} %get-tuple-element.411), channel_id=1, source_target_pairs={{0,16},{8,24},{16,0},{24,8},{1,17},{9,25},{17,1},{25,9},{2,18},{10... | collective-permute-start | bytes 983048 | tf_op jit(solution)/shard_map/ppermute | solution.py:677
  282.9 24.5 %collective-permute-start.34 = (bf16[64,2560]{1,0:T(8,128)(2,1)}, bf16[64,2560]{1,0:T(8,128)(2,1)}, u32[]{:S(2)}, u32[]{:S(2)}) collective-permute-start(bf16[64,2560]{1,0:T(8,128)(2,1)} %get-tuple-element.409), channel_id=1, source_target_pairs={{0,8},{8,16},{16,24},{24,0},{1,9},{9,17},{17,25},{25,1},{2,10},{10... | collective-permute-start | bytes 983048 | tf_op jit(solution)/shard_map/ppermute | solution.py:677
  283.9 25.5 %collective-permute-start.37 = (bf16[1024,512]{1,0:T(8,128)(2,1)}, bf16[1024,512]{1,0:T(8,128)(2,1)}, u32[]{:S(2)}, u32[]{:S(2)}) collective-permute-start(bf16[1024,512]{1,0:T(8,128)(2,1)} %get-tuple-element.339), channel_id=1, source_target_pairs={{0,1},{1,0},{2,3},{3,2},{4,5},{5,4},{6,7},{7,6},{8,9},{9,8},{10,11... | collective-permute-start | bytes 3145736 | tf_op jit(solution)/shard_map/ppermute | solution.py:638
  328.1 11.0 %collective-permute-start.42 = (bf16[80,1536]{1,0:T(8,128)(2,1)S(1)}, bf16[80,1536]{1,0:T(8,128)(2,1)S(1)}, u32[]{:S(2)}, u32[]{:S(2)}) collective-permute-start(bf16[80,1536]{1,0:T(8,128)(2,1)S(1)} %get-tuple-element.426), channel_id=1, source_target_pairs={{0,24},{8,0},{16,8},{24,16},{1,25},{9,1},{17,9},{25,17},{2,26},{10... | collective-permute-start | bytes 737288 | tf_op jit(solution)/shard_map/ppermute | solution.py:677
  330.5 13.2 %collective-permute-start.41 = (bf16[80,1536]{1,0:T(8,128)(2,1)S(1)}, bf16[80,1536]{1,0:T(8,128)(2,1)S(1)}, u32[]{:S(2)}, u32[]{:S(2)}) collective-permute-start(bf16[80,1536]{1,0:T(8,128)(2,1)S(1)} %get-tuple-element.425), channel_id=1, source_target_pairs={{0,16},{8,24},{16,0},{24,8},{1,17},{9,25},{17,1},{25,9},{2,18},{10... | collective-permute-start | bytes 737288 | tf_op jit(solution)/shard_map/ppermute | solution.py:677
  332.0 11.7 %collective-permute-start.40 = (bf16[80,1536]{1,0:T(8,128)(2,1)S(1)}, bf16[80,1536]{1,0:T(8,128)(2,1)S(1)}, u32[]{:S(2)}, u32[]{:S(2)}) collective-permute-start(bf16[80,1536]{1,0:T(8,128)(2,1)S(1)} %get-tuple-element.424), channel_id=1, source_target_pairs={{0,8},{8,16},{16,24},{24,0},{1,9},{9,17},{17,25},{25,1},{2,10},{10... | collective-permute-start | bytes 737288 | tf_op jit(solution)/shard_map/ppermute | solution.py:677
  344.1 23.1 %collective-permute-start.44 = (bf16[32,4096]{1,0:T(8,128)(2,1)S(1)}, bf16[32,4096]{1,0:T(8,128)(2,1)S(1)}, u32[]{:S(2)}, u32[]{:S(2)}) collective-permute-start(bf16[32,4096]{1,0:T(8,128)(2,1)S(1)} %get-tuple-element.422), channel_id=1, source_target_pairs={{0,4},{1,5},{2,6},{3,7},{4,0},{5,1},{6,2},{7,3},{8,12},{9,13},{10,... | collective-permute-start | bytes 786440 | tf_op jit(solution)/shard_map/ppermute | solution.py:677
  344.7 22.5 %collective-permute-start.43 = (bf16[32,4096]{1,0:T(8,128)(2,1)S(1)}, bf16[32,4096]{1,0:T(8,128)(2,1)S(1)}, u32[]{:S(2)}, u32[]{:S(2)}) collective-permute-start(bf16[32,4096]{1,0:T(8,128)(2,1)S(1)} %get-tuple-element.421), channel_id=1, source_target_pairs={{0,2},{1,3},{2,4},{3,5},{4,6},{5,7},{6,0},{7,1},{8,10},{9,11},{10,... | collective-permute-start | bytes 786440 | tf_op jit(solution)/shard_map/ppermute | solution.py:677
  367.8 11.5 %collective-permute-start.47 = (bf16[16,4096]{1,0:T(8,128)(2,1)S(1)}, bf16[16,4096]{1,0:T(8,128)(2,1)S(1)}, u32[]{:S(2)}, u32[]{:S(2)}) collective-permute-start(bf16[16,4096]{1,0:T(8,128)(2,1)S(1)} %add_convert_fusion.6), channel_id=1, source_target_pairs={{0,4},{1,5},{2,6},{3,7},{4,0},{5,1},{6,2},{7,3},{8,12},{9,13},{10,... | collective-permute-start | bytes 393224 | tf_op jit(solution)/shard_map/ppermute | solution.py:689
  379.4 15.8 %collective-permute-start.49 = (bf16[64,4096]{1,0:T(8,128)(2,1)S(1)}, bf16[64,4096]{1,0:T(8,128)(2,1)S(1)}, u32[]{:S(2)}, u32[]{:S(2)}) collective-permute-start(bf16[64,4096]{1,0:T(8,128)(2,1)S(1)} %constant_dynamic-update-slice_fusion.4), channel_id=1, source_target_pairs={{0,8},{8,16},{16,24},{24,0},{1,9},{9,17},{17,25},{25,1},{2,10},{10... | collective-permute-start | bytes 1572872 | tf_op jit(solution)/shard_map/ppermute | solution.py:689
  380.1 24.3 %collective-permute-start.50 = (bf16[64,4096]{1,0:T(8,128)(2,1)S(1)}, bf16[64,4096]{1,0:T(8,128)(2,1)S(1)}, u32[]{:S(2)}, u32[]{:S(2)}) collective-permute-start(bf16[64,4096]{1,0:T(8,128)(2,1)S(1)} %constant_dynamic-update-slice_fusion.4), channel_id=1, source_target_pairs={{0,16},{8,24},{16,0},{24,8},{1,17},{9,25},{17,1},{25,9},{2,18},{10... | collective-permute-start | bytes 1572872 | tf_op jit(solution)/shard_map/ppermute | solution.py:689
  381.6 22.9 %collective-permute-start.51 = (bf16[64,4096]{1,0:T(8,128)(2,1)S(1)}, bf16[64,4096]{1,0:T(8,128)(2,1)S(1)}, u32[]{:S(2)}, u32[]{:S(2)}) collective-permute-start(bf16[64,4096]{1,0:T(8,128)(2,1)S(1)} %constant_dynamic-update-slice_fusion.4), channel_id=1, source_target_pairs={{0,24},{8,0},{16,8},{24,16},{1,25},{9,1},{17,9},{25,17},{2,26},{10... | collective-permute-start | bytes 1572872 | tf_op jit(solution)/shard_map/ppermute | solution.py:689
  384.2 20.4 %collective-permute-start.52 = (bf16[256,512]{1,0:T(8,128)(2,1)S(1)}, bf16[256,512]{1,0:T(8,128)(2,1)S(1)}, u32[]{:S(2)}, u32[]{:S(2)}) collective-permute-start(bf16[256,512]{1,0:T(8,128)(2,1)S(1)} %copy-done.24), channel_id=1, source_target_pairs={{0,6},{1,7},{2,0},{3,1},{4,2},{5,3},{6,4},{7,5},{8,14},{9,15},{10,... | collective-permute-start | bytes 786440 | tf_op jit(solution)/shard_map/ppermute | solution.py:628
  389.4 20.9 %collective-permute-start.53 = (bf16[256,512]{1,0:T(8,128)(2,1)S(1)}, bf16[256,512]{1,0:T(8,128)(2,1)S(1)}, u32[]{:S(2)}, u32[]{:S(2)}) collective-permute-start(bf16[256,512]{1,0:T(8,128)(2,1)S(1)} %copy-done.23), channel_id=1, source_target_pairs={{0,4},{1,5},{2,6},{3,7},{4,0},{5,1},{6,2},{7,3},{8,12},{9,13},{10,... | collective-permute-start | bytes 786440 | tf_op jit(solution)/shard_map/ppermute | solution.py:628
  395.2 15.0 %collective-permute-start.54 = (bf16[256,512]{1,0:T(8,128)(2,1)S(1)}, bf16[256,512]{1,0:T(8,128)(2,1)S(1)}, u32[]{:S(2)}, u32[]{:S(2)}) collective-permute-start(bf16[256,512]{1,0:T(8,128)(2,1)S(1)} %copy-done.22), channel_id=1, source_target_pairs={{0,2},{1,3},{2,4},{3,5},{4,6},{5,7},{6,0},{7,1},{8,10},{9,11},{10,... | collective-permute-start | bytes 786440 | tf_op jit(solution)/shard_map/ppermute | solution.py:628
  (46 other events, 237.0 us)
